TPU v7x, 512 devices: a whole 4x4x16 slice. The times are simulated.
512 devices in a mesh: dp: 16 (over y_lo, x, core), tensor: 32 (over y_hi, z).
Axes of the slice: x: 4, y: 4 (y_hi: 2, y_lo: 2; y = y_hi * 2 + y_lo), z: 16, core: 2. Of those that a mesh axis runs over, the one named last changes fastest.
Arguments:
- tokens: bfloat16 [4096, 12288], P('dp', 'tensor'), may hold values from -6 to 6
- w_blocks: bfloat16 [192, 1536, 128], P('tensor'), may hold values from -0.15625 to 0.15625
- pattern: int32 [192, 12], P('tensor'), may hold values from 0 to 95, as said below
- low_left: bfloat16 [12288, 256], P('tensor'), may hold values from -0.0546875 to 0.0546875
- low_right: bfloat16 [256, 24576], P(None, 'tensor'), may hold values from -0.375 to 0.375
- grad_out: bfloat16 [4096, 24576], P('dp', 'tensor'), may hold values from -6 to 6
Outputs:
- hidden: bfloat16 [4096, 24576], P('dp', 'tensor')
- grad_tokens: float32 [4096, 12288], P('dp', 'tensor')
- grad_blocks: float32 [192, 1536, 128], P('tensor', 'dp')
- grad_left: float32 [12288, 256], P('tensor', 'dp')
- grad_right: float32 [256, 24576], P('dp', 'tensor')
Inputs may be any that keep to these rules, and one draw needn't show every extreme that they name: Each row pattern[j] holds 12 distinct block rows. With n the tensor axis's size, m = 12288 / (128 * n) block rows to a shard of the features and s = j // (24576 / (128 * n)) the shard holding block column j, every entry lies in feature shard s or in shard s XOR 2**k for some k, and one entry of the row is s m + (j mod m).
All inputs are finite; a program needn't handle non-finite values.
Results may differ from a plain program's by a relative error of at most 0.023.
Values may be sent and summed in bfloat16 or wider, within the bound.
A program may use at most 64 MiB of HBM per device.

v0:
```python
import math

import jax
import jax.numpy as jnp
from jax import lax
from jax.sharding import PartitionSpec as P

BLOCK = 128
NNZ = 12


def swapped(block, axis, stride):
    count = lax.axis_size(axis)
    route = []
    for low in range(count):
        high = low | 1 << stride
        if high != low and high < count:
            route += [(low, high), (high, low)]
    return lax.ppermute(block, axis, route)


def candidate_slots(block_rows, shard_index, shard_blocks, levels_count):
    owners = block_rows // shard_blocks
    distance = jnp.bitwise_xor(owners, shard_index)
    ranked = jnp.zeros_like(block_rows)
    for section in range(levels_count):
        ranked = ranked + jnp.where(distance == 1 << section, section + 1, 0).astype(jnp.int32)
    return ranked * shard_blocks + block_rows % shard_blocks


def per_device(tokens, w_blocks, pattern, low_left, low_right, grad_out):
    shard_index = lax.axis_index("tensor")
    levels_count = lax.axis_size("tensor").bit_length() - 1
    token_rows = tokens.shape[0]
    shard_width = tokens.shape[1]
    shard_blocks = shard_width // BLOCK
    columns = w_blocks.shape[0]
    every_shard = lax.all_gather(tokens, "tensor", axis=1, tiled=True)
    pieces = [tokens]
    for section in range(levels_count):
        partner = jnp.bitwise_xor(shard_index, 1 << section)
        pieces.append(lax.dynamic_slice_in_dim(every_shard, partner * shard_width, shard_width, 1))
    slot_count = (levels_count + 1) * shard_blocks
    candidates = jnp.concatenate(pieces, axis=1).reshape(token_rows, slot_count, BLOCK)
    slot_index = candidate_slots(pattern, shard_index, shard_blocks, levels_count).reshape(-1)
    chosen = jnp.take(candidates, slot_index, axis=1).reshape(token_rows, columns, NNZ, BLOCK)
    weights = w_blocks.reshape(columns, NNZ, BLOCK, BLOCK)
    sparse_part = jnp.einsum("tjkb,jkbo->tjo", chosen, weights, preferred_element_type=jnp.float32)
    sparse_part = sparse_part.reshape(token_rows, columns * BLOCK)
    code_terms = jnp.dot(tokens, low_left, preferred_element_type=jnp.float32)
    low_codes = lax.psum(code_terms, "tensor").astype(jnp.bfloat16)
    pre_act = sparse_part + jnp.dot(low_codes, low_right, preferred_element_type=jnp.float32)
    hidden_full, pullback = jax.vjp(jax.nn.gelu, pre_act)
    hidden = hidden_full.astype(jnp.bfloat16)
    pre_grad = pullback(grad_out.astype(jnp.float32))[0].astype(jnp.bfloat16)
    back_terms = jnp.einsum("to,ro->tr", pre_grad, low_right, preferred_element_type=jnp.float32)
    back_codes = lax.psum(back_terms, "tensor").astype(jnp.bfloat16)
    pre_grad_cols = pre_grad.reshape(token_rows, columns, BLOCK)
    grad_scale = 1.0 / math.sqrt(token_rows * lax.axis_size("dp"))
    products = jnp.einsum(
        "tjo,jkbo->tjkb", pre_grad_cols, weights, preferred_element_type=jnp.float32
    )
    products = products.reshape(token_rows, columns * NNZ, BLOCK)
    collected = (
        jnp.zeros((token_rows, slot_count, BLOCK), jnp.float32).at[:, slot_index].add(products)
    )
    flattened = collected.reshape(token_rows, slot_count * BLOCK)
    summed = flattened[:, :shard_width]
    for section in range(levels_count):
        outgoing = flattened[:, (section + 1) * shard_width : (section + 2) * shard_width]
        summed = summed + swapped(outgoing, "tensor", section)
    summed = summed + jnp.einsum(
        "tr,ir->ti", back_codes, low_left, preferred_element_type=jnp.float32
    )
    term_blocks = jnp.einsum(
        "tjkb,tjo->jkbo", chosen, pre_grad_cols, preferred_element_type=jnp.float32
    )
    term_blocks = (
        (term_blocks * grad_scale).reshape(columns, NNZ * BLOCK, BLOCK).astype(jnp.bfloat16)
    )
    term_left = (
        jnp.einsum("ti,tr->ir", tokens, back_codes, preferred_element_type=jnp.float32) * grad_scale
    )
    term_right = (
        jnp.einsum("tr,to->ro", low_codes, pre_grad, preferred_element_type=jnp.float32)
        * grad_scale
    )
    term_left, term_right = (term_left.astype(jnp.bfloat16), term_right.astype(jnp.bfloat16))
    grad_blocks = lax.psum_scatter(term_blocks, "dp", scatter_dimension=1, tiled=True).astype(
        jnp.float32
    )
    grad_left = lax.psum_scatter(term_left, "dp", scatter_dimension=1, tiled=True).astype(
        jnp.float32
    )
    grad_right = lax.psum_scatter(term_right, "dp", scatter_dimension=0, tiled=True).astype(
        jnp.float32
    )
    return (hidden, summed, grad_blocks, grad_left, grad_right)


def solution(mesh):
    in_specs = (
        P("dp", "tensor"),
        P("tensor", None, None),
        P("tensor", None),
        P("tensor", None),
        P(None, "tensor"),
        P("dp", "tensor"),
    )
    out_specs = (
        P("dp", "tensor"),
        P("dp", "tensor"),
        P("tensor", "dp", None),
        P("tensor", "dp"),
        P("dp", "tensor"),
    )
    return jax.shard_map(
        per_device, mesh=mesh, in_specs=in_specs, out_specs=out_specs, check_vma=False
    )
```

profile of v0, /device:TPU:1, one launch (start us, length us, event | category | flops | bytes accessed | tf_op | source)
XLA Modules:
  0.0 578.9 jit_solution(15502551951739118985)
XLA Ops:
  7.2 0.0 copy-start
  7.2 0.0 all-gather.2.cloned.1.call-start
  7.2 1.9 copy.19
  9.1 0.0 all-gather.2.cloned.1.call-update
  9.1 0.0 reduce-scatter.6.cloned.1.call-start
  9.2 0.7 compare_and_fusion
  9.9 0.1 reshape.71
  10.0 1.9 fusion.32
  12.0 0.9 constant_dynamic-update-slice_fusion
  12.9 131.5 %all-reduce.2 = bf16[256,256]{1,0:T(8,128)(2,1)} all-reduce(f32[256,256]{1,0:T(8,128)} %fusion.32), channel_id=1, replica_groups=mesh['dp'=16,'tensor'=32] {'tensor'}, use_global_device_ids=true, to_apply=%region_0.1 | all-reduce | flops 65536 | bytes 393216 | tf_op jit(solution)/shard_map/psum | solution.py:51
  144.4 44.1 %all-gather.2.cloned.1.call-done = bf16[256,12288]{0,1:T(8,128)(2,1)} async-done(((bf16[256,384]{0,1:T(8,128)(2,1)}), bf16[256,12288]{0,1:T(8,128)(2,1)}) %all-gather.2.cloned.1.call-update) | async-done | bytes 6291472 | tf_op jit(solution)/shard_map/all_gather | solution.py:38
  188.5 0.9 dynamic-slice_dynamic-update-slice_fusion.4
  189.5 0.9 dynamic-slice_dynamic-update-slice_fusion.3
  190.4 0.9 dynamic-slice_dynamic-update-slice_fusion.2
  191.4 0.9 dynamic-slice_dynamic-update-slice_fusion.1
  192.3 0.9 dynamic-slice_dynamic-update-slice_fusion
  193.3 1.0 copy-done.2
  194.3 1.7 copy.20
  196.0 5.5 gather_fusion
  201.5 6.6 %copy.21 = bf16[256,6,12,128]{0,3,2,1:T(8,128)(2,1)} copy(bf16[256,6,12,128]{3,0,2,1:T(8,128)(2,1)} %bitcast.47) | data formatting | bytes 9437184 | tf_op jit(solution)/shard_map/jit(_take)/gather | solution.py:46
  208.2 0.0 copy-done
  208.2 3.5 fusion.1
  211.7 1.2 copy.24
  212.9 3.0 fusion.9
  215.8 0.0 copy-done.5
  215.8 0.3 fusion.34
  216.1 118.6 %all-reduce.3 = bf16[256,256]{1,0:T(8,128)(2,1)S(1)} all-reduce(f32[256,256]{1,0:T(8,128)S(1)} %fusion.34), channel_id=1, replica_groups=mesh['dp'=16,'tensor'=32] {'tensor'}, use_global_device_ids=true, to_apply=%region_2.3 | all-reduce | flops 65536 | bytes 393216 | tf_op jit(solution)/shard_map/psum | solution.py:57
  334.8 0.9 fusion.6
  335.7 0.0 reduce-scatter.6.cloned.1.call-update
  335.7 0.0 reduce-scatter.8.cloned.1.call-start
  335.8 1.1 fusion.4
  336.8 0.0 reduce-scatter.8.cloned.1.call-update
  336.9 0.0 reduce-scatter.4.cloned.1.call-start
  336.9 0.2 copy.25
  337.1 5.2 multiply_convert_fusion
  342.3 0.0 reduce-scatter.4.cloned.1.call-update
  342.3 5.1 fusion.33
  347.4 1.7 broadcast_in_dim.31
  349.1 23.9 %scatter_fusion = f32[256,18,128]{2,0,1:T(8,128)} fusion(f32[256,18,128]{2,0,1:T(8,128)} %broadcast_in_dim.31, s32[72]{0:T(128)S(1)} %fusion.27, f32[72,256,128]{2,1,0:T(8,128)} %bitcast.46), kind=kCustom, calls=%fused_computation.1 | custom fusion | flops 2359296 | bytes 28311840 | tf_op jit(solution)/shard_map/scatter-add | solution.py:65
  373.0 3.1 copy.27
  376.0 2.6 fusion.31
  378.7 1.9 copy.45
  380.6 1.9 copy.48
  382.5 1.9 copy.47
  384.4 0.9 copy.46
  385.3 0.9 copy.49
  386.3 4.2 collective-permute-start.4
  390.5 1.9 collective-permute-start.1
  392.4 1.9 collective-permute-start.2
  394.3 8.1 %collective-permute-start.3 = (f32[256,384]{1,0:T(8,128)}, f32[256,384]{1,0:T(8,128)}, u32[]{:S(2)}, u32[]{:S(2)}) collective-permute-start(f32[256,384]{1,0:T(8,128)} %copy.48), channel_id=1, source_target_pairs={{0,8},{8,0},{1,9},{9,1},{2,10},{10,2},{3,11},{11,3},{4,12},{12,4},... | collective-permute-start | bytes 1179656 | tf_op jit(solution)/shard_map/ppermute | solution.py:19
  402.5 1.9 collective-permute-start
  404.4 0.2 copy.44
  404.6 23.5 %reduce-scatter.6.cloned.1.call-done = bf16[384,16]{0,1:T(8,128)(2,1)} async-done(((bf16[384,256]{0,1:T(8,128)(2,1)}), bf16[384,16]{0,1:T(8,128)(2,1)}) %reduce-scatter.6.cloned.1.call-update) | async-done | bytes 12304 | tf_op jit(solution)/shard_map/reduce_scatter | solution.py:92
  428.1 1.3 convert_element_type.49
  429.4 0.0 collective-permute-done.4
  429.4 0.0 collective-permute-done.1
  429.4 1.4 collective-permute-done.2
  430.8 0.0 collective-permute-done.3
  430.8 0.0 collective-permute-done
  430.8 2.5 add_add_fusion
  433.3 65.3 %reduce-scatter.8.cloned.1.call-done = bf16[16,768]{1,0:T(8,128)(2,1)} async-done(((bf16[256,768]{1,0:T(8,128)(2,1)}), bf16[16,768]{1,0:T(8,128)(2,1)}) %reduce-scatter.8.cloned.1.call-update) | async-done | bytes 24592 | tf_op jit(solution)/shard_map/reduce_scatter | solution.py:95
  498.6 1.4 convert_element_type.51
  500.0 70.7 %reduce-scatter.4.cloned.1.call-done = bf16[6,96,128]{2,1,0:T(8,128)(2,1)} async-done(((bf16[6,1536,128]{2,1,0:T(8,128)(2,1)}), bf16[6,96,128]{2,1,0:T(8,128)(2,1)}) %reduce-scatter.4.cloned.1.call-update) | async-done | bytes 147472 | tf_op jit(solution)/shard_map/reduce_scatter | solution.py:89
  570.7 1.6 convert_element_type.46
  (10 shorter events, 0.0 us)
Async XLA Ops:
  7.2 201.0 %copy-start = (bf16[6,1536,128]{2,1,0:T(8,128)(2,1)S(1)}, bf16[6,1536,128]{2,1,0:T(8,128)(2,1)}, u32[]{:S(2)}) copy-start(bf16[6,1536,128]{2,1,0:T(8,128)(2,1)} %param.7) | copy-start | bytes 7077892
  7.2 181.3 %all-gather.2.cloned.1.call-start = ((), (), s32[]{:S(2)}) async-start(), calls=%async_computation.3 | async-start | bytes 6488064 | tf_op jit(solution)/shard_map/all_gather | solution.py:38
  9.1 418.9 %reduce-scatter.6.cloned.1.call-start = ((), (), s32[]{:S(2)}) async-start(), calls=%async_computation.5 | async-start | bytes 208896 | tf_op jit(solution)/shard_map/reduce_scatter | solution.py:92
  193.3 1.0 copy-start.2
  208.2 4.7 copy-start.4
  212.9 3.0 copy-start.5
  212.9 121.9 %copy-start.1 = (bf16[256,384]{1,0:T(8,128)(2,1)S(1)}, bf16[256,384]{1,0:T(8,128)(2,1)}, u32[]{:S(2)}) copy-start(bf16[256,384]{1,0:T(8,128)(2,1)} %param.6) | copy-start | bytes 589828
  334.8 2.1 copy-start.3
  335.7 162.9 %reduce-scatter.8.cloned.1.call-start = ((), (), s32[]{:S(2)}) async-start(), calls=%async_computation.6 | async-start | bytes 417792 | tf_op jit(solution)/shard_map/reduce_scatter | solution.py:95
  336.9 233.8 %reduce-scatter.4.cloned.1.call-start = ((), (), s32[]{:S(2)}) async-start(), calls=%async_computation.4 | async-start | bytes 2506752 | tf_op jit(solution)/shard_map/reduce_scatter | solution.py:89
  386.3 43.1 %collective-permute-start.4 = (f32[256,384]{1,0:T(8,128)}, f32[256,384]{1,0:T(8,128)S(1)}, u32[]{:S(2)}, u32[]{:S(2)}) collective-permute-start(f32[256,384]{1,0:T(8,128)} %copy.49), channel_id=1, source_target_pairs={{0,16},{16,0},{1,17},{17,1},{2,18},{18,2},{3,19},{19,3},{4,20},{20... | collective-permute-start | bytes 1179656 | tf_op jit(solution)/shard_map/ppermute | solution.py:19
  390.5 38.9 %collective-permute-start.1 = (f32[256,384]{1,0:T(8,128)}, f32[256,384]{1,0:T(8,128)}, u32[]{:S(2)}, u32[]{:S(2)}) collective-permute-start(f32[256,384]{1,0:T(8,128)} %copy.46), channel_id=1, source_target_pairs={{0,2},{2,0},{1,3},{3,1},{4,6},{6,4},{5,7},{7,5},{8,10},{10,8},{9,1... | collective-permute-start | bytes 1179656 | tf_op jit(solution)/shard_map/ppermute | solution.py:19
  392.4 38.4 %collective-permute-start.2 = (f32[256,384]{1,0:T(8,128)}, f32[256,384]{1,0:T(8,128)}, u32[]{:S(2)}, u32[]{:S(2)}) collective-permute-start(f32[256,384]{1,0:T(8,128)} %copy.47), channel_id=1, source_target_pairs={{0,4},{4,0},{1,5},{5,1},{2,6},{6,2},{3,7},{7,3},{8,12},{12,8},{9,1... | collective-permute-start | bytes 1179656 | tf_op jit(solution)/shard_map/ppermute | solution.py:19
  394.3 36.5 %collective-permute-start.3 = (f32[256,384]{1,0:T(8,128)}, f32[256,384]{1,0:T(8,128)}, u32[]{:S(2)}, u32[]{:S(2)}) collective-permute-start(f32[256,384]{1,0:T(8,128)} %copy.48), channel_id=1, source_target_pairs={{0,8},{8,0},{1,9},{9,1},{2,10},{10,2},{3,11},{11,3},{4,12},{12,4},... | collective-permute-start | bytes 1179656 | tf_op jit(solution)/shard_map/ppermute | solution.py:19
  402.5 28.3 %collective-permute-start = (f32[256,384]{1,0:T(8,128)}, f32[256,384]{1,0:T(8,128)}, u32[]{:S(2)}, u32[]{:S(2)}) collective-permute-start(f32[256,384]{1,0:T(8,128)} %copy.45), channel_id=1, source_target_pairs={{0,1},{1,0},{2,3},{3,2},{4,5},{5,4},{6,7},{7,6},{8,9},{9,8},{10,11... | collective-permute-start | bytes 1179656 | tf_op jit(solution)/shard_map/ppermute | solution.py:19
Sparse Core Ops, SparseCore 0:
  11.7 176.7 all-gather.1
  335.8 92.1 reduce-scatter.5
  431.1 67.4 reduce-scatter.7
  501.3 69.3 reduce-scatter.3
where the time goes:
time: 581 us; the launch traced here: 579 us
  blocking collectives  250 us (43%)
  waiting for transfers between devices  205 us (35%)
  local copies, waits for them, and re-layouts  39.1 us (7%)
  other arithmetic  28.9 us (5%)
  matrix products  23.4 us (4%)
  starting transfers between devices  18.3 us (3%)
  between operations  13.9 us (2%)
    psum x1, blocking collectives, per_device(): low_codes = lax.psum(code_terms, 'tensor').astype(jnp.bfloat16)  132 us
    psum x1, blocking collectives, per_device(): back_codes = lax.psum(back_terms, 'tensor').astype(jnp.bfloat16)  119 us
    reduce_scatter x1, waiting for transfers between devices, per_device(): lax.psum_scatter(term_blocks, 'dp', scatter_dimension=1, tiled=True)  70.7 us
    reduce_scatter x1, waiting for transfers between devices, per_device(): lax.psum_scatter(term_right, 'dp', scatter_dimension=0, tiled=True)  65.3 us
    all_gather x1, waiting for transfers between devices, per_device(): every_shard = lax.all_gather(tokens, 'tensor', axis=1, tiled=True)  44.1 us
    scatter-add x1, other arithmetic, per_device(): jnp.zeros((token_rows, slot_count, BLOCK), jnp.float32).at[:, slot_index]  23.9 us
    reduce_scatter x1, waiting for transfers between devices, per_device(): lax.psum_scatter(term_left, 'dp', scatter_dimension=1, tiled=True)  23.5 us
    ppermute x5, starting transfers between devices, swapped(): return lax.ppermute(block, axis, route)  18.1 us
  transfers between devices with their start and end apart: 9, of which 5 were waited for; matrix products, arithmetic and copies ran while one was open for 10% of the time, Pallas kernels for 0%

commit v1 on v0

v1 whole, which is shorter than its diff:
```python
import functools
import math

import jax
import jax.numpy as jnp
from jax import lax
from jax.experimental import pallas as pl
from jax.experimental.pallas import tpu as pltpu
from jax.sharding import PartitionSpec as P

MESH = pl.DeviceIdType.MESH
BF, F32 = jnp.bfloat16, jnp.float32
BLOCK = 128
NNZ = 12
TOK = 256
MB = 3
COLS = 6
LEVELS = 6
SLOTS = MB * LEVELS
RANK = 256
HID = COLS * BLOCK
FEAT = MB * BLOCK
CHUNKS = 6
GROUPS = 2
GCOLS = COLS // GROUPS
CHIPS = 8
TENSOR_PEERS = (1, 2, 4, 12, 16)
CHIP_MASKS = tuple(range(1, CHIPS))
GELU_C = math.sqrt(2.0 / math.pi)
GELU_A = 0.044715


def dot(a, b):
    return jnp.dot(a, b, preferred_element_type=F32)


class Sems:
    def __init__(self, send, recv):
        self.send, self.recv, self.used = send, recv, 0

    def copy(self, src, dst, **device):
        i = self.used
        self.used += 1
        return pltpu.make_async_remote_copy(
            src_ref=src, dst_ref=dst, send_sem=self.send.at[i], recv_sem=self.recv.at[i],
            device_id=device, device_id_type=MESH,
        )


NUM_SEMS = 160


def kernel(
    grad_scale, tokens, w, pat, left, right, gout,
    hidden, gtok, gblk, glt, gright,
    cand, cand_t, wd, wd_t, pre, pg, left_t, right_t,
    acc, stage128, stage64, stage32, stage16, stagec,
    rb128, rb64, rb32, rb16, rbc, rc128, rc64, rc32, rc16, rcc,
    codes, back, gsend, rx, g4, g0,
    tb, tb_rc, tb_s, tb_r, tr, tr_rc, tr_s, tr_r, tl, tl_rc, tl_s, tl_r,
    send_sem, recv_sem,
):
    s = lax.axis_index("tensor")
    d = lax.axis_index("dp")
    core = lax.rem(d, 2)
    chip = d // 2
    other = 1 - core
    sems = Sems(send_sem, recv_sem)
    pending = []

    def launch(src, dst, **device):
        c = sems.copy(src, dst, **device)
        c.start()
        pending.append(c)
        return c

    barrier = pltpu.get_barrier_semaphore()
    for m in TENSOR_PEERS:
        pl.semaphore_signal(barrier, inc=1, device_id={"tensor": s ^ m}, device_id_type=MESH)
    pl.semaphore_signal(barrier, inc=1, device_id={"dp": d ^ 1}, device_id_type=MESH)
    for m in CHIP_MASKS:
        pl.semaphore_signal(barrier, inc=1, device_id={"dp": d ^ (2 * m)}, device_id_type=MESH)
    for i in range(MB):
        cand[i] = tokens[:, i * BLOCK : (i + 1) * BLOCK]
    pl.semaphore_wait(barrier, len(TENSOR_PEERS) + 1 + len(CHIP_MASKS))

    def part(c):
        i, h = c // 2, c % 2
        return i, pl.ds(h * 128, 128)

    four = []
    for c in range(CHUNKS):
        i, rows = part(c)
        four.append(launch(cand.at[i, rows], cand.at[9 + i, rows], tensor=s ^ 4))
    own = cand.at[pl.ds(0, MB)]
    sixteen = launch(own, cand.at[pl.ds(15, MB)], tensor=s ^ 16)
    two = launch(own, cand.at[pl.ds(6, MB)], tensor=s ^ 2)
    one = launch(own, cand.at[pl.ds(3, MB)], tensor=s ^ 1)
    relayed = []

    def relay(c):
        i, rows = part(c)
        four[c].wait_recv()
        relayed.append(launch(cand.at[9 + i, rows], cand.at[12 + i, rows], tensor=s ^ 12))

    bit = lambda n: lax.rem(lax.shift_right_logical(s, n), 2)
    b16, b1, b2, b3 = bit(4), bit(0), bit(1), bit(3)
    b4 = bit(2) ^ b3
    off = [0]
    for b, h in ((b16, 128), (b1, 64), (b2, 32), (b4, 16)):
        off.append(off[-1] + b * h)
    col = pl.multiple_of(b3 * 128, 128)
    row_steps = ((16, b16, 128, stage128), (1, b1, 64, stage64), (2, b2, 32, stage32), (4, b4, 16, stage16))

    def rows_at(start, size):
        return pl.ds(pl.multiple_of(start, 16), size)

    class AllReduce:
        def __init__(self, bufs, out):
            self.bufs, self.out, self.flying = bufs, out, None

        def scatter_send(self, i):
            if i < 4:
                mask, b, h, stage = row_steps[i]
                stage[...] = acc[rows_at(off[i] + (1 - b) * h, h), :].astype(BF)
            else:
                mask, stage = 12, stagec
                ocol = pl.multiple_of((1 - b3) * 128, 128)
                stage[...] = acc[rows_at(off[4], 16), pl.ds(ocol, 128)].astype(BF)
            self.flying = launch(stage, self.bufs[i], tensor=s ^ mask)

        def scatter_recv(self, i):
            self.flying.wait()
            pending[:] = [c for c in pending if c is not self.flying]
            if i < 4:
                h = row_steps[i][2]
                keep = rows_at(off[i + 1], h)
                acc[keep, :] = acc[keep, :] + self.bufs[i][...].astype(F32)
            else:
                keep = rows_at(off[4], 16)
                self.out[keep, pl.ds(col, 128)] = (
                    acc[keep, pl.ds(col, 128)] + self.bufs[4][...].astype(F32)
                ).astype(BF)

        def gather_send(self, i):
            if i == 0:
                view, mask = self.out.at[rows_at(off[4], 16), pl.ds(col, 128)], 12
            else:
                k = 4 - i
                mask, _, h, _ = row_steps[k]
                view = self.out.at[rows_at(off[k + 1], h)]
            self.flying = launch(view, view, tensor=s ^ mask)

        def gather_recv(self):
            self.flying.wait_recv()

        def step(self, n):
            if n < 5:
                self.scatter_recv(n)
                if n < 4:
                    self.scatter_send(n + 1)
                else:
                    self.gather_send(0)
            else:
                self.gather_recv()
                if n < 9:
                    self.gather_send(n - 4)

    ar = AllReduce((rb128, rb64, rb32, rb16, rbc), codes)
    acc[...] = dot(tokens[...], left[...])
    ar.scatter_send(0)

    def dense(first, last):
        def body(slot, carry):
            level = slot // MB
            mask = lax.shift_right_logical(lax.shift_left(jnp.int32(1), level), 1)
            row = (s ^ mask) * MB + lax.rem(slot, MB)
            for j in range(COLS):
                k = jnp.int32(0)
                found = jnp.int32(0)
                for q in range(NNZ):
                    hit = pat[j, q] == row
                    k = jnp.where(hit, q, k)
                    found = jnp.where(hit, 1, found)
                block = jnp.where(found > 0, w[j, k], jnp.zeros((BLOCK, BLOCK), BF))
                wd[slot, :, j * BLOCK : (j + 1) * BLOCK] = block
                wd_t[slot, j * BLOCK : (j + 1) * BLOCK, :] = block.T
            return carry

        lax.fori_loop(first, last, body, 0)

    def turned(first, last):
        def body(slot, carry):
            cand_t[slot] = cand[slot].T
            return carry

        lax.fori_loop(first, last, body, 0)

    def forward(slots, start=None):
        def body(n, carry):
            columns = pl.ds(pl.multiple_of(n * 256, 256), 256)
            total = start(columns) if start is not None else pre[:, columns]
            for p in range(0, len(slots), 2):
                pair = slots[p : p + 2]
                x = jnp.concatenate([cand[q] for q in pair], axis=1)
                y = jnp.concatenate([wd[q, :, columns] for q in pair], axis=0)
                total = total + dot(x, y)
            pre[:, columns] = total
            return carry

        lax.fori_loop(0, HID // 256, body, 0)

    dense(0, 6)
    ar.step(0)
    dense(6, 12)
    ar.step(1)
    relay(0)
    dense(12, 18)
    ar.step(2)
    relay(1)
    left_t[...] = left[...].T
    right_t[...] = right[...].T
    turned(0, 3)
    ar.step(3)
    relay(2)
    sixteen.wait_recv()
    turned(15, 18)
    ar.step(4)
    relay(3)
    one.wait_recv()
    two.wait_recv()
    turned(3, 9)
    ar.step(5)
    relay(4)
    ar.step(6)
    relay(5)
    forward((0, 1, 2, 15, 16, 17, 3, 4, 5, 6, 7, 8), lambda columns: jnp.zeros((TOK, 256), F32))
    ar.step(7)
    turned(9, 12)
    forward((9, 10, 11))
    ar.step(8)
    for c in range(CHUNKS):
        relayed[c].wait_recv()
        if c == 3:
            ar.step(9)
    turned(12, 15)

    def activate(n, carry):
        columns = pl.ds(pl.multiple_of(n * 256, 256), 256)
        u = pre[:, columns]
        u = u + dot(jnp.concatenate([cand[12], cand[13]], axis=1),
                    jnp.concatenate([wd[12, :, columns], wd[13, :, columns]], axis=0))
        u = u + dot(cand[14], wd[14, :, columns])
        u = u + dot(codes[...], right[:, columns])
        uu = u * u
        t = jnp.tanh(GELU_C * (u + GELU_A * (uu * u)))
        hidden[:, columns] = (0.5 * u * (1.0 + t)).astype(BF)
        slope = 0.5 * (1.0 + t) + 0.5 * u * (1.0 - t * t) * (GELU_C * (1.0 + 3.0 * GELU_A * uu))
        pg[:, columns] = (gout[:, columns].astype(F32) * slope).astype(BF)
        return carry

    lax.fori_loop(0, HID // 256, activate, 0)

    def term(slot):
        return dot(pg[...], wd_t[slot])

    far = []
    for i in range(MB):
        gsend[12 + i] = term(12 + i).astype(BF)
        far.append(launch(gsend.at[12 + i], rx.at[12 + i], tensor=s ^ 12))
    ar = AllReduce((rc128, rc64, rc32, rc16, rcc), back)
    acc[...] = dot(pg[...], right_t[...])
    ar.scatter_send(0)

    def near(level, mask):
        def body(i, carry):
            gsend[MB * level + i] = term(MB * level + i).astype(BF)
            return carry

        lax.fori_loop(0, MB, body, 0)
        view = pl.ds(MB * level, MB)
        return launch(gsend.at[view], rx.at[view], tensor=s ^ mask)

    nears = [near(5, 16), near(2, 2), near(1, 1)]

    def g4_body(i, carry):
        g4[i] = term(9 + i)
        return carry

    lax.fori_loop(0, MB, g4_body, 0)

    def slot_of(p):
        apart = (p // MB) ^ s
        level = jnp.int32(0)
        for n in range(LEVELS - 1):
            level = level + (apart == (1 << n)).astype(jnp.int32) * (n + 1)
        return level * MB + lax.rem(p, MB)

    def blocks(group):
        def body(n, carry):
            j = group * GCOLS + n
            g = pg[:, pl.ds(pl.multiple_of(j * BLOCK, BLOCK), BLOCK)]
            for k in range(NNZ):
                x = (dot(cand_t[slot_of(pat[j, k])], g) * grad_scale).astype(BF)
                row = 0
                while row < BLOCK:
                    at = k * BLOCK + row
                    piece, inner = at // 96, at % 96
                    size = min(96 - inner, BLOCK - row)
                    tb[j, piece // 2, piece % 2, inner : inner + size, :] = x[row : row + size]
                    row += size
            return carry

        lax.fori_loop(0, GCOLS, body, 0)
        view = pl.ds(group * GCOLS, GCOLS)
        return launch(tb.at[view, :, other], tb_rc.at[view], dp=d ^ 1)

    def spread(sent, received):
        return [launch(sent(chip ^ m), received(m), dp=d ^ (2 * m)) for m in CHIP_MASKS]

    def blocks_sum(group, copy):
        copy.wait_recv()

        def body(c, carry):
            for n in range(GCOLS):
                j = group * GCOLS + n
                tb_s[group, c, n] = (tb[j, c, core].astype(F32) + tb_rc[j, c].astype(F32)).astype(BF)
            return carry

        lax.fori_loop(0, CHIPS, body, 0)
        return spread(lambda c: tb_s.at[group, c], lambda m: tb_r.at[group, m])

    def flat_sum(mine, theirs, out, copy, received):
        copy.wait_recv()

        def body(c, carry):
            out[c] = (mine[c, core].astype(F32) + theirs[c].astype(F32)).astype(BF)
            return carry

        lax.fori_loop(0, CHIPS, body, 0)
        return spread(lambda c: out.at[c], lambda m: received.at[m])

    def far_relay(i):
        far[i].wait_recv()
        gsend[9 + i] = (g4[i] + rx[12 + i].astype(F32)).astype(BF)
        return launch(gsend.at[9 + i], rx.at[9 + i], tensor=s ^ 4)

    core0 = blocks(0)
    ar.step(0)
    core1 = blocks(1)
    t = (dot(codes[...].T, pg[...]) * grad_scale).astype(BF)
    for c in range(CHIPS):
        for h in range(2):
            r = (2 * c + h) * 16
            tr[c, h] = t[r : r + 16]
    core_r = launch(tr.at[:, other], tr_rc, dp=d ^ 1)
    ar.step(1)
    eight0 = blocks_sum(0, core0)
    nears.append(far_relay(0))
    ar.step(2)
    eight1 = blocks_sum(1, core1)
    nears.append(far_relay(1))
    ar.step(3)
    eight_r = flat_sum(tr, tr_rc, tr_s, core_r, tr_r)
    nears.append(far_relay(2))
    ar.step(4)

    def g0_body(i, carry):
        g0[i] = term(i)
        return carry

    lax.fori_loop(0, MB, g0_body, 0)
    for n in range(5, 10):
        ar.step(n)
    t = (dot(back[...].T, tokens[...]) * grad_scale).astype(BF)
    for c in range(CHIPS):
        for h in range(2):
            r = (2 * c + h) * 16
            tl[c, h] = t[r : r + 16]
    core_l = launch(tl.at[:, other], tl_rc, dp=d ^ 1)
    eight_l = flat_sum(tl, tl_rc, tl_s, core_l, tl_r)

    def sum_flat(own_view, received, copies, out):
        total = own_view[...].astype(F32)
        for m, c in zip(CHIP_MASKS, copies):
            c.wait_recv()
            total = total + received[m].astype(F32)
        out[...] = total

    for group, copies in ((0, eight0), (1, eight1)):
        for c in copies:
            c.wait_recv()

        def body(n, carry, group=group):
            total = tb_s[group, chip, n].astype(F32)
            for m in CHIP_MASKS:
                total = total + tb_r[group, m, n].astype(F32)
            gblk[group * GCOLS + n] = total
            return carry

        lax.fori_loop(0, GCOLS, body, 0)
    sum_flat(tr_s.at[chip], tr_r, eight_r, gright)
    for c in nears:
        c.wait_recv()
    low = dot(back[...], left_t[...])
    for i in range(MB):
        total = g0[i] + low[:, i * BLOCK : (i + 1) * BLOCK]
        for level in (1, 2, 3, 5):
            total = total + rx[MB * level + i].astype(F32)
        gtok[:, i * BLOCK : (i + 1) * BLOCK] = total
    sum_flat(tl_s.at[chip], tl_r, eight_l, glt)
    for c in pending:
        c.wait_send()


def per_device(tokens, w_blocks, pattern, low_left, low_right, grad_out):
    grad_scale = 1.0 / math.sqrt(TOK * lax.axis_size("dp"))
    vmem = pl.BlockSpec(memory_space=pltpu.VMEM)
    smem = pl.BlockSpec(memory_space=pltpu.SMEM)
    V = pltpu.VMEM
    ar_bufs = [V((h, RANK), BF) for h in (128, 64, 32, 16)] + [V((16, 128), BF)]
    scratch = [
        V((SLOTS, TOK, BLOCK), BF), V((SLOTS, BLOCK, TOK), BF),
        V((SLOTS, BLOCK, HID), BF), V((SLOTS, HID, BLOCK), BF),
        V((TOK, HID), F32), V((TOK, HID), BF), V((RANK, FEAT), BF), V((HID, RANK), BF),
        V((TOK, RANK), F32), *ar_bufs, *ar_bufs, *ar_bufs,
        V((TOK, RANK), BF), V((TOK, RANK), BF),
        V((SLOTS, TOK, BLOCK), BF), V((SLOTS, TOK, BLOCK), BF),
        V((MB, TOK, BLOCK), F32), V((MB, TOK, BLOCK), F32),
        V((COLS, CHIPS, 2, 96, BLOCK), BF), V((COLS, CHIPS, 96, BLOCK), BF),
        V((GROUPS, CHIPS, GCOLS, 96, BLOCK), BF), V((GROUPS, CHIPS, GCOLS, 96, BLOCK), BF),
        V((CHIPS, 2, 16, HID), BF), V((CHIPS, 16, HID), BF), V((CHIPS, 16, HID), BF), V((CHIPS, 16, HID), BF),
        V((CHIPS, 2, 16, FEAT), BF), V((CHIPS, 16, FEAT), BF), V((CHIPS, 16, FEAT), BF), V((CHIPS, 16, FEAT), BF),
        pltpu.SemaphoreType.DMA((NUM_SEMS,)), pltpu.SemaphoreType.DMA((NUM_SEMS,)),
    ]
    out_shape = (
        jax.ShapeDtypeStruct((TOK, HID), BF),
        jax.ShapeDtypeStruct((TOK, FEAT), F32),
        jax.ShapeDtypeStruct((COLS, 96, BLOCK), F32),
        jax.ShapeDtypeStruct((16, FEAT), F32),
        jax.ShapeDtypeStruct((16, HID), F32),
    )
    hidden, gtok, gblk, glt, gright = pl.pallas_call(
        functools.partial(kernel, grad_scale),
        name="pixelfly",
        out_shape=out_shape,
        in_specs=[vmem, vmem, smem, vmem, vmem, vmem],
        out_specs=(vmem,) * 5,
        scratch_shapes=scratch,
        compiler_params=pltpu.CompilerParams(
            collective_id=0, has_side_effects=True, vmem_limit_bytes=48 << 20
        ),
        cost_estimate=pl.CostEstimate(flops=3 << 30, bytes_accessed=6 << 20, transcendentals=TOK * HID),
    )(tokens, w_blocks.reshape(COLS, NNZ, BLOCK, BLOCK), pattern, low_left, low_right, grad_out)
    return hidden, gtok, gblk, glt.T, gright


def solution(mesh):
    in_specs = (
        P("dp", "tensor"),
        P("tensor", None, None),
        P("tensor", None),
        P("tensor", None),
        P(None, "tensor"),
        P("dp", "tensor"),
    )
    out_specs = (
        P("dp", "tensor"),
        P("dp", "tensor"),
        P("tensor", "dp", None),
        P("tensor", "dp"),
        P("dp", "tensor"),
    )
    return jax.shard_map(
        per_device, mesh=mesh, in_specs=in_specs, out_specs=out_specs, check_vma=False
    )
```

time: 581 us -> 145 us (0.25)
  blocking collectives: 250 us -> 0 us
  waiting for transfers between devices: 205 us -> 0 us
  Pallas kernels: 0 us -> 135 us
  local copies, waits for them, and re-layouts: 39.1 us -> 9.62 us
  other arithmetic: 28.9 us -> 0 us
  matrix products: 23.4 us -> 0 us
  starting transfers between devices: 18.3 us -> 0 us
  between operations: 13.9 us -> 0.66 us
    psum x2 -> x0, blocking collectives: 250 us -> none  [the longest x1 132 us: per_device(): low_codes = lax.psum(code_terms, 'tensor').astype(jnp.bfloat16)]
    reduce_scatter x3 -> x0, waiting for transfers between devices: 160 us -> none  [the longest x1 70.7 us: per_device(): lax.psum_scatter(term_blocks, 'dp', scatter_dimension=1, tiled=True)]
    pallas_call x0 -> x1, Pallas kernels: none -> 135 us  [per_device(): pl.pallas_call(functools.partial(kernel, grad_scale), name='pixelfly', ou...]
    all_gather x1 -> x0, waiting for transfers between devices: 44.1 us -> none  [per_device(): every_shard = lax.all_gather(tokens, 'tensor', axis=1, tiled=True)]
    scatter-add x1 -> x0, other arithmetic: 23.9 us -> none  [per_device(): jnp.zeros((token_rows, slot_count, BLOCK), jnp.float32).at[:, slot_index]]
    dot_general x9 -> x0, matrix products: 23.4 us -> none  [the longest x1 5.17 us: per_device(): jnp.einsum('tjkb,tjo->jkbo', chosen, pre_grad_cols, preferred_element_typ...]
    ppermute x5 -> x0, starting transfers between devices: 18.1 us -> none  [swapped(): return lax.ppermute(block, axis, route)]
    gather x2 -> x0, local copies, waits for them, and re-layouts: 12.2 us -> none  [per_device(): jnp.take(candidates, slot_index, axis=1)]
  transfers between devices with their start and end apart: 9 -> 0, of which waited for: 5 -> 0; matrix products, arithmetic and copies ran while one was open for 10% -> 0% of each run, Pallas kernels for 0% -> 0%
where the time goes in v1:
time: 145 us
  Pallas kernels  135 us (93%)
  local copies, waits for them, and re-layouts  9.62 us (7%)
    pallas_call x1, Pallas kernels, per_device(): pl.pallas_call(functools.partial(kernel, grad_scale), name='pixelfly', ou...  135 us
    unnamed x17, local copies, waits for them, and re-layouts  9.62 us

profile of v1, /device:TPU:1, one launch (start us, length us, event | category | flops | bytes accessed | tf_op | source)
XLA Modules:
  0.0 145.0 jit_solution(9292881886992313097)
XLA Ops:
  0.6 0.0 copy-start
  0.6 1.7 %copy-done = bf16[6,1536,128]{2,1,0:T(8,128)(2,1)S(1)} copy-done((bf16[6,1536,128]{2,1,0:T(8,128)(2,1)S(1)}, bf16[6,1536,128]{2,1,0:T(8,128)(2,1)}, u32[]{:S(2)}) %copy-start) | copy-done | bytes 2359320
  2.3 0.0 copy-start.1
  2.3 1.0 copy-done.1
  3.3 0.0 copy-start.2
  3.3 1.0 copy-done.2
  4.3 0.0 copy-start.3
  4.3 0.9 copy-done.3
  5.2 0.0 copy-start.4
  5.2 0.9 copy-done.4
  6.1 0.0 copy-start.5
  6.1 0.7 copy-done.5
  6.8 134.8 %pixelfly.1 = (bf16[256,768]{1,0:T(8,128)(2,1)S(1)}, f32[256,384]{1,0:T(8,128)S(1)}, f32[6,96,128]{2,1,0:T(8,128)S(1)}, f32[16,384]{1,0:T(8,128)S(1)}, f32[16,768]{1,0:T(8,128)S(1)}) custom-call(bf16[256,384]{1,0:T(8,128)(2,1)S(1)} %copy-done.3, bf16[6,12,128,128]{3,2,1,0:T(8,128)(2,1)S(1)} %bitcast.3, s32[6,12]{1,0:T(8,128)S(1)} %copy-done.5, ...), custom_call_target="tpu_custom_call" | custom-call | flops 3221225472 | bytes 6291456 | tf_op jit(solution)/shard_map/pixelfly/pallas_call | solution.py:443
  141.6 0.7 copy.16
  142.3 0.7 copy.17
  143.1 0.7 copy.18
  143.8 0.6 copy.19
  144.4 0.6 copy.20
Async XLA Ops:
  0.6 1.7 %copy-start = (bf16[6,1536,128]{2,1,0:T(8,128)(2,1)S(1)}, bf16[6,1536,128]{2,1,0:T(8,128)(2,1)}, u32[]{:S(2)}) copy-start(bf16[6,1536,128]{2,1,0:T(8,128)(2,1)} %param.7) | copy-start | bytes 7077892
  2.3 1.0 copy-start.1
  3.3 1.0 copy-start.2
  4.3 0.9 copy-start.3
  5.2 0.9 copy-start.4
  6.1 0.7 copy-start.5

commit v2 on v1

--- a/solution.py
+++ b/solution.py
@@ -24,7 +24,9 @@
 GROUPS = 2
 GCOLS = COLS // GROUPS
 CHIPS = 8
-TENSOR_PEERS = (1, 2, 4, 12, 16)
+NEAR_GROUP = (1, 2, 3, 16, 17, 18, 19)
+FAR_GROUP = (4, 8, 12)
+TENSOR_PEERS = NEAR_GROUP + FAR_GROUP
 CHIP_MASKS = tuple(range(1, CHIPS))
 GELU_C = math.sqrt(2.0 / math.pi)
 GELU_A = 0.044715
@@ -51,11 +53,11 @@
 
 
 def kernel(
-    grad_scale, tokens, w, pat, left, right, gout,
+    grad_scale, tokens_hbm, w_hbm, pat_hbm, left_hbm, right_hbm, gout_hbm,
     hidden, gtok, gblk, glt, gright,
+    w, pat, left, right, gout, load_sem,
     cand, cand_t, wd, wd_t, pre, pg, left_t, right_t,
-    acc, stage128, stage64, stage32, stage16, stagec,
-    rb128, rb64, rb32, rb16, rbc, rc128, rc64, rc32, rc16, rcc,
+    acc, acc2, sa_f, sa_b, sb_f, sb_b, ra_f, ra_b, rb_f, rb_b,
     codes, back, gsend, rx, g4, g0,
     tb, tb_rc, tb_s, tb_r, tr, tr_rc, tr_s, tr_r, tl, tl_rc, tl_s, tl_r,
     send_sem, recv_sem,
@@ -80,16 +82,88 @@
     pl.semaphore_signal(barrier, inc=1, device_id={"dp": d ^ 1}, device_id_type=MESH)
     for m in CHIP_MASKS:
         pl.semaphore_signal(barrier, inc=1, device_id={"dp": d ^ (2 * m)}, device_id_type=MESH)
-    for i in range(MB):
-        cand[i] = tokens[:, i * BLOCK : (i + 1) * BLOCK]
+
+    def fetch(n, src, dst):
+        c = pltpu.make_async_copy(src, dst, load_sem.at[n])
+        c.start()
+        return c
+
+    loads = [fetch(i, tokens_hbm.at[:, pl.ds(i * BLOCK, BLOCK)], cand.at[i]) for i in range(MB)]
+    loads.append(fetch(3, left_hbm, left))
+    pat_load = fetch(4, pat_hbm, pat)
+    w_load = fetch(5, w_hbm, w)
+    right_load = fetch(6, right_hbm, right)
+    gout_load = fetch(7, gout_hbm, gout)
+    for c in loads:
+        c.wait()
+
+    def tokens():
+        return jnp.concatenate([cand[i] for i in range(MB)], axis=1)
+
+    acc[...] = dot(tokens(), left[...])
+    sa_f[...] = acc[...].astype(BF)
     pl.semaphore_wait(barrier, len(TENSOR_PEERS) + 1 + len(CHIP_MASKS))
 
     def part(c):
         i, h = c // 2, c % 2
         return i, pl.ds(h * 128, 128)
 
+    bit = lambda v, n: lax.rem(lax.shift_right_logical(v, n), 2)
+    near_row = lambda v: pl.multiple_of(32 * (bit(v, 0) + 2 * bit(v, 1) + 4 * bit(v, 4)), 32)
+    far_row = lambda v: pl.multiple_of(16 * bit(v, 2), 16)
+    far_col = lambda v: pl.multiple_of(128 * bit(v, 3), 128)
+
+    class AllReduce:
+        def __init__(self, total, near_stage, far_stage, near_in, far_in, out):
+            self.total, self.near_stage, self.far_stage = total, near_stage, far_stage
+            self.near_in, self.far_in, self.out = near_in, far_in, out
+
+        def start(self):
+            self.flying = [
+                launch(self.near_stage.at[pl.ds(near_row(s ^ m), 32)], self.near_in.at[n], tensor=s ^ m)
+                for n, m in enumerate(NEAR_GROUP)
+            ]
+
+        def arrived(self):
+            for c in self.flying:
+                c.wait_recv()
+
+        def step(self, n):
+            self.arrived()
+            rows = pl.ds(near_row(s), 32)
+            piece = self.out.at[pl.ds(pl.multiple_of(near_row(s) + far_row(s), 16), 16), pl.ds(far_col(s), 128)]
+            if n == 0:
+                part = self.total[rows, :]
+                for m in range(len(NEAR_GROUP)):
+                    part = part + self.near_in[m].astype(F32)
+                self.total[rows, :] = part
+                self.far_stage[...] = part.astype(BF)
+                self.flying = [
+                    launch(
+                        self.far_stage.at[pl.ds(far_row(s ^ m), 16), pl.ds(far_col(s ^ m), 128)],
+                        self.far_in.at[i], tensor=s ^ m,
+                    )
+                    for i, m in enumerate(FAR_GROUP)
+                ]
+            elif n == 1:
+                part = self.total[
+                    pl.ds(pl.multiple_of(near_row(s) + far_row(s), 16), 16), pl.ds(far_col(s), 128)
+                ]
+                for m in range(len(FAR_GROUP)):
+                    part = part + self.far_in[m].astype(F32)
+                piece[...] = part.astype(BF)
+                self.flying = [launch(piece, piece, tensor=s ^ m) for m in FAR_GROUP]
+            elif n == 2:
+                view = self.out.at[rows]
+                self.flying = [launch(view, view, tensor=s ^ m) for m in NEAR_GROUP]
+
     four = []
-    for c in range(CHUNKS):
+    for c in range(2):
+        i, rows = part(c)
+        four.append(launch(cand.at[i, rows], cand.at[9 + i, rows], tensor=s ^ 4))
+    ar = AllReduce(acc, sa_f, sb_f, ra_f, rb_f, codes)
+    ar.start()
+    for c in range(2, CHUNKS):
         i, rows = part(c)
         four.append(launch(cand.at[i, rows], cand.at[9 + i, rows], tensor=s ^ 4))
     own = cand.at[pl.ds(0, MB)]
@@ -102,73 +176,6 @@
         i, rows = part(c)
         four[c].wait_recv()
         relayed.append(launch(cand.at[9 + i, rows], cand.at[12 + i, rows], tensor=s ^ 12))
-
-    bit = lambda n: lax.rem(lax.shift_right_logical(s, n), 2)
-    b16, b1, b2, b3 = bit(4), bit(0), bit(1), bit(3)
-    b4 = bit(2) ^ b3
-    off = [0]
-    for b, h in ((b16, 128), (b1, 64), (b2, 32), (b4, 16)):
-        off.append(off[-1] + b * h)
-    col = pl.multiple_of(b3 * 128, 128)
-    row_steps = ((16, b16, 128, stage128), (1, b1, 64, stage64), (2, b2, 32, stage32), (4, b4, 16, stage16))
-
-    def rows_at(start, size):
-        return pl.ds(pl.multiple_of(start, 16), size)
-
-    class AllReduce:
-        def __init__(self, bufs, out):
-            self.bufs, self.out, self.flying = bufs, out, None
-
-        def scatter_send(self, i):
-            if i < 4:
-                mask, b, h, stage = row_steps[i]
-                stage[...] = acc[rows_at(off[i] + (1 - b) * h, h), :].astype(BF)
-            else:
-                mask, stage = 12, stagec
-                ocol = pl.multiple_of((1 - b3) * 128, 128)
-                stage[...] = acc[rows_at(off[4], 16), pl.ds(ocol, 128)].astype(BF)
-            self.flying = launch(stage, self.bufs[i], tensor=s ^ mask)
-
-        def scatter_recv(self, i):
-            self.flying.wait()
-            pending[:] = [c for c in pending if c is not self.flying]
-            if i < 4:
-                h = row_steps[i][2]
-                keep = rows_at(off[i + 1], h)
-                acc[keep, :] = acc[keep, :] + self.bufs[i][...].astype(F32)
-            else:
-                keep = rows_at(off[4], 16)
-                self.out[keep, pl.ds(col, 128)] = (
-                    acc[keep, pl.ds(col, 128)] + self.bufs[4][...].astype(F32)
-                ).astype(BF)
-
-        def gather_send(self, i):
-            if i == 0:
-                view, mask = self.out.at[rows_at(off[4], 16), pl.ds(col, 128)], 12
-            else:
-                k = 4 - i
-                mask, _, h, _ = row_steps[k]
-                view = self.out.at[rows_at(off[k + 1], h)]
-            self.flying = launch(view, view, tensor=s ^ mask)
-
-        def gather_recv(self):
-            self.flying.wait_recv()
-
-        def step(self, n):
-            if n < 5:
-                self.scatter_recv(n)
-                if n < 4:
-                    self.scatter_send(n + 1)
-                else:
-                    self.gather_send(0)
-            else:
-                self.gather_recv()
-                if n < 9:
-                    self.gather_send(n - 4)
-
-    ar = AllReduce((rb128, rb64, rb32, rb16, rbc), codes)
-    acc[...] = dot(tokens[...], left[...])
-    ar.scatter_send(0)
 
     def dense(first, last):
         def body(slot, carry):
@@ -210,41 +217,38 @@
 
         lax.fori_loop(0, HID // 256, body, 0)
 
-    dense(0, 6)
+    pat_load.wait()
+    w_load.wait()
+    dense(0, 4)
+    relay(0)
     ar.step(0)
-    dense(6, 12)
+    dense(4, 8)
+    relay(1)
+    dense(8, 12)
+    relay(2)
     ar.step(1)
-    relay(0)
-    dense(12, 18)
-    ar.step(2)
-    relay(1)
+    dense(12, 15)
+    relay(3)
+    dense(15, 18)
+    right_load.wait()
     left_t[...] = left[...].T
+    relay(4)
     right_t[...] = right[...].T
     turned(0, 3)
-    ar.step(3)
-    relay(2)
     sixteen.wait_recv()
     turned(15, 18)
-    ar.step(4)
-    relay(3)
+    relay(5)
+    ar.step(2)
     one.wait_recv()
     two.wait_recv()
     turned(3, 9)
-    ar.step(5)
-    relay(4)
-    ar.step(6)
-    relay(5)
     forward((0, 1, 2, 15, 16, 17, 3, 4, 5, 6, 7, 8), lambda columns: jnp.zeros((TOK, 256), F32))
-    ar.step(7)
     turned(9, 12)
     forward((9, 10, 11))
-    ar.step(8)
+    ar.step(3)
+    gout_load.wait()
     for c in range(CHUNKS):
         relayed[c].wait_recv()
-        if c == 3:
-            ar.step(9)
-    turned(12, 15)
-
     def activate(n, carry):
         columns = pl.ds(pl.multiple_of(n * 256, 256), 256)
         u = pre[:, columns]
@@ -261,16 +265,20 @@
 
     lax.fori_loop(0, HID // 256, activate, 0)
 
+    acc2[...] = dot(pg[...], right_t[...])
+    sa_b[...] = acc2[...].astype(BF)
+    ar = AllReduce(acc2, sa_b, sb_b, ra_b, rb_b, back)
+    ar.start()
+
     def term(slot):
         return dot(pg[...], wd_t[slot])
 
     far = []
     for i in range(MB):
         gsend[12 + i] = term(12 + i).astype(BF)
-        far.append(launch(gsend.at[12 + i], rx.at[12 + i], tensor=s ^ 12))
-    ar = AllReduce((rc128, rc64, rc32, rc16, rcc), back)
-    acc[...] = dot(pg[...], right_t[...])
-    ar.scatter_send(0)
+        for h in range(2):
+            rows = pl.ds(h * 128, 128)
+            far.append(launch(gsend.at[12 + i, rows], rx.at[12 + i, rows], tensor=s ^ 12))
 
     def near(level, mask):
         def body(i, carry):
@@ -340,44 +348,47 @@
         lax.fori_loop(0, CHIPS, body, 0)
         return spread(lambda c: out.at[c], lambda m: received.at[m])
 
-    def far_relay(i):
-        far[i].wait_recv()
-        gsend[9 + i] = (g4[i] + rx[12 + i].astype(F32)).astype(BF)
-        return launch(gsend.at[9 + i], rx.at[9 + i], tensor=s ^ 4)
-
+    def far_relay(c):
+        i, rows = part(c)
+        far[c].wait_recv()
+        gsend[9 + i, rows] = (g4[i, rows] + rx[12 + i, rows].astype(F32)).astype(BF)
+        nears.append(launch(gsend.at[9 + i, rows], rx.at[9 + i, rows], tensor=s ^ 4))
+
+    def flat_parts(out, t):
+        for c in range(CHIPS):
+            for h in range(2):
+                r = (2 * c + h) * 16
+                out[c, h] = t[r : r + 16]
+
+    turned(12, 15)
     core0 = blocks(0)
     ar.step(0)
+    far_relay(0)
     core1 = blocks(1)
-    t = (dot(codes[...].T, pg[...]) * grad_scale).astype(BF)
-    for c in range(CHIPS):
-        for h in range(2):
-            r = (2 * c + h) * 16
-            tr[c, h] = t[r : r + 16]
+    flat_parts(tr, (dot(codes[...].T, pg[...]) * grad_scale).astype(BF))
     core_r = launch(tr.at[:, other], tr_rc, dp=d ^ 1)
+    eight0 = blocks_sum(0, core0)
+    far_relay(1)
     ar.step(1)
-    eight0 = blocks_sum(0, core0)
-    nears.append(far_relay(0))
-    ar.step(2)
     eight1 = blocks_sum(1, core1)
-    nears.append(far_relay(1))
-    ar.step(3)
+    far_relay(2)
     eight_r = flat_sum(tr, tr_rc, tr_s, core_r, tr_r)
-    nears.append(far_relay(2))
-    ar.step(4)
 
     def g0_body(i, carry):
         g0[i] = term(i)
         return carry
 
     lax.fori_loop(0, MB, g0_body, 0)
-    for n in range(5, 10):
-        ar.step(n)
-    t = (dot(back[...].T, tokens[...]) * grad_scale).astype(BF)
-    for c in range(CHIPS):
-        for h in range(2):
-            r = (2 * c + h) * 16
-            tl[c, h] = t[r : r + 16]
+    far_relay(3)
+    ar.step(2)
+    far_relay(4)
+    far_relay(5)
+    ar.step(3)
+    flat_parts(tl, (dot(back[...].T, tokens()) * grad_scale).astype(BF))
     core_l = launch(tl.at[:, other], tl_rc, dp=d ^ 1)
+    low = dot(back[...], left_t[...])
+    for i in range(MB):
+        g0[i] = g0[i] + low[:, i * BLOCK : (i + 1) * BLOCK]
     eight_l = flat_sum(tl, tl_rc, tl_s, core_l, tl_r)
 
     def sum_flat(own_view, received, copies, out):
@@ -402,9 +413,8 @@
     sum_flat(tr_s.at[chip], tr_r, eight_r, gright)
     for c in nears:
         c.wait_recv()
-    low = dot(back[...], left_t[...])
     for i in range(MB):
-        total = g0[i] + low[:, i * BLOCK : (i + 1) * BLOCK]
+        total = g0[i]
         for level in (1, 2, 3, 5):
             total = total + rx[MB * level + i].astype(F32)
         gtok[:, i * BLOCK : (i + 1) * BLOCK] = total
@@ -416,14 +426,17 @@
 def per_device(tokens, w_blocks, pattern, low_left, low_right, grad_out):
     grad_scale = 1.0 / math.sqrt(TOK * lax.axis_size("dp"))
     vmem = pl.BlockSpec(memory_space=pltpu.VMEM)
-    smem = pl.BlockSpec(memory_space=pltpu.SMEM)
+    hbm = pl.BlockSpec(memory_space=pl.ANY)
     V = pltpu.VMEM
-    ar_bufs = [V((h, RANK), BF) for h in (128, 64, 32, 16)] + [V((16, 128), BF)]
     scratch = [
+        V((COLS, NNZ, BLOCK, BLOCK), BF), pltpu.SMEM((COLS, NNZ), jnp.int32),
+        V((FEAT, RANK), BF), V((RANK, HID), BF), V((TOK, HID), BF), pltpu.SemaphoreType.DMA((8,)),
         V((SLOTS, TOK, BLOCK), BF), V((SLOTS, BLOCK, TOK), BF),
         V((SLOTS, BLOCK, HID), BF), V((SLOTS, HID, BLOCK), BF),
         V((TOK, HID), F32), V((TOK, HID), BF), V((RANK, FEAT), BF), V((HID, RANK), BF),
-        V((TOK, RANK), F32), *ar_bufs, *ar_bufs, *ar_bufs,
+        V((TOK, RANK), F32), V((TOK, RANK), F32), V((TOK, RANK), BF), V((TOK, RANK), BF),
+        V((32, RANK), BF), V((32, RANK), BF), V((7, 32, RANK), BF), V((7, 32, RANK), BF),
+        V((3, 16, 128), BF), V((3, 16, 128), BF),
         V((TOK, RANK), BF), V((TOK, RANK), BF),
         V((SLOTS, TOK, BLOCK), BF), V((SLOTS, TOK, BLOCK), BF),
         V((MB, TOK, BLOCK), F32), V((MB, TOK, BLOCK), F32),
@@ -444,11 +457,11 @@
         functools.partial(kernel, grad_scale),
         name="pixelfly",
         out_shape=out_shape,
-        in_specs=[vmem, vmem, smem, vmem, vmem, vmem],
+        in_specs=[hbm] * 6,
         out_specs=(vmem,) * 5,
         scratch_shapes=scratch,
         compiler_params=pltpu.CompilerParams(
-            collective_id=0, has_side_effects=True, vmem_limit_bytes=48 << 20
+            collective_id=0, has_side_effects=True, vmem_limit_bytes=56 << 20
         ),
         cost_estimate=pl.CostEstimate(flops=3 << 30, bytes_accessed=6 << 20, transcendentals=TOK * HID),
     )(tokens, w_blocks.reshape(COLS, NNZ, BLOCK, BLOCK), pattern, low_left, low_right, grad_out)

time: 145 us -> 121 us (0.83)
  Pallas kernels: 135 us -> 112 us
  local copies, waits for them, and re-layouts: 9.62 us -> 7.99 us
    pallas_call x1, Pallas kernels: 135 us -> 112 us  [per_device(): pl.pallas_call(functools.partial(kernel, grad_scale), name='pixelfly', ou...]
    unnamed x17 -> x5, local copies, waits for them, and re-layouts: 9.62 us -> 7.99 us
where the time goes in v2:
time: 121 us
  Pallas kernels  112 us (93%)
  local copies, waits for them, and re-layouts  7.99 us (7%)
    pallas_call x1, Pallas kernels, per_device(): pl.pallas_call(functools.partial(kernel, grad_scale), name='pixelfly', ou...  112 us
    unnamed x5, local copies, waits for them, and re-layouts  7.99 us

profile of v2, /device:TPU:1, one launch (start us, length us, event | category | flops | bytes accessed | tf_op | source)
XLA Modules:
  0.0 120.6 jit_solution(10183006188772321662)
XLA Ops:
  0.6 112.0 %pixelfly.1 = (bf16[256,768]{1,0:T(8,128)(2,1)}, f32[256,384]{1,0:T(8,128)}, f32[6,96,128]{2,1,0:T(8,128)}, f32[16,384]{1,0:T(8,128)}, f32[16,768]{1,0:T(8,128)}) custom-call(bf16[256,384]{1,0:T(8,128)(2,1)} %tokens_hbm.1, bf16[6,12,128,128]{3,2,1,0:T(8,128)(2,1)} %bitcast.3, s32[6,12]{1,0:T(8,128)} %pat_hbm.1, bf16[384,256]{1,0:T(8,128)(2,1)} %left_hbm.1, ...), custom_call_target="tpu_custom_call" | custom-call | flops 3221225472 | bytes 6291456 | tf_op jit(solution)/shard_map/pixelfly/pallas_call | solution.py:456
  112.6 1.8 %copy.16 = bf16[256,768]{1,0:T(8,128)(2,1)} copy(bf16[256,768]{1,0:T(8,128)(2,1)} %get-tuple-element.20) | data formatting | bytes 786432
  114.4 1.8 %copy.17 = f32[256,384]{1,0:T(8,128)} copy(f32[256,384]{1,0:T(8,128)} %get-tuple-element.21) | data formatting | bytes 786432
  116.2 1.7 %copy.18 = f32[6,96,128]{2,1,0:T(8,128)} copy(f32[6,96,128]{2,1,0:T(8,128)} %get-tuple-element.22) | data formatting | bytes 589824
  117.8 1.3 %copy.19 = f32[384,16]{0,1:T(8,128)} copy(f32[384,16]{0,1:T(8,128)} %bitcast.2) | data formatting | bytes 49152
  119.2 1.4 %copy.20 = f32[16,768]{1,0:T(8,128)} copy(f32[16,768]{1,0:T(8,128)} %get-tuple-element.24) | data formatting | bytes 98304

commit v3 on v2

--- a/solution.py
+++ b/solution.py
@@ -20,13 +20,14 @@
 RANK = 256
 HID = COLS * BLOCK
 FEAT = MB * BLOCK
-CHUNKS = 6
 GROUPS = 2
 GCOLS = COLS // GROUPS
 CHIPS = 8
-NEAR_GROUP = (1, 2, 3, 16, 17, 18, 19)
-FAR_GROUP = (4, 8, 12)
-TENSOR_PEERS = NEAR_GROUP + FAR_GROUP
+NEAR_GROUP = (19, 18, 17, 16, 3, 2, 1)
+FAR_GROUP = (8, 4, 12)
+TENSOR_PEERS = tuple(
+    near ^ far ^ y for far in (8, 12, 4, 0) for y in (16, 0) for near in (3, 2, 1, 0) if near ^ far ^ y
+)
 CHIP_MASKS = tuple(range(1, CHIPS))
 GELU_C = math.sqrt(2.0 / math.pi)
 GELU_A = 0.044715
@@ -57,7 +58,7 @@
     hidden, gtok, gblk, glt, gright,
     w, pat, left, right, gout, load_sem,
     cand, cand_t, wd, wd_t, pre, pg, left_t, right_t,
-    acc, acc2, sa_f, sa_b, sb_f, sb_b, ra_f, ra_b, rb_f, rb_b,
+    acc, acc2, sa_f, sa_b, ra_f, ra_b,
     codes, back, gsend, rx, g4, g0,
     tb, tb_rc, tb_s, tb_r, tr, tr_rc, tr_s, tr_r, tl, tl_rc, tl_s, tl_r,
     send_sem, recv_sem,
@@ -76,6 +77,17 @@
         pending.append(c)
         return c
 
+    def fetch(n, src, dst):
+        c = pltpu.make_async_copy(src, dst, load_sem.at[n])
+        c.start()
+        return c
+
+    loads = [fetch(i, tokens_hbm.at[:, pl.ds(i * BLOCK, BLOCK)], cand.at[i]) for i in range(MB)]
+    loads.append(fetch(3, left_hbm, left))
+    pat_load = fetch(4, pat_hbm, pat)
+    w_load = fetch(5, w_hbm, w)
+    right_load = fetch(6, right_hbm, right)
+    gout_load = fetch(7, gout_hbm, gout)
     barrier = pltpu.get_barrier_semaphore()
     for m in TENSOR_PEERS:
         pl.semaphore_signal(barrier, inc=1, device_id={"tensor": s ^ m}, device_id_type=MESH)
@@ -83,99 +95,66 @@
     for m in CHIP_MASKS:
         pl.semaphore_signal(barrier, inc=1, device_id={"dp": d ^ (2 * m)}, device_id_type=MESH)
 
-    def fetch(n, src, dst):
-        c = pltpu.make_async_copy(src, dst, load_sem.at[n])
-        c.start()
-        return c
-
-    loads = [fetch(i, tokens_hbm.at[:, pl.ds(i * BLOCK, BLOCK)], cand.at[i]) for i in range(MB)]
-    loads.append(fetch(3, left_hbm, left))
-    pat_load = fetch(4, pat_hbm, pat)
-    w_load = fetch(5, w_hbm, w)
-    right_load = fetch(6, right_hbm, right)
-    gout_load = fetch(7, gout_hbm, gout)
     for c in loads:
         c.wait()
 
     def tokens():
         return jnp.concatenate([cand[i] for i in range(MB)], axis=1)
 
+    def in_pieces(out, x):
+        for p in range(32):
+            row = 32 * ((p & 3) + 4 * (p >> 4)) + 16 * ((p >> 2) & 1)
+            column = 128 * ((p >> 3) & 1)
+            out[p] = x[row : row + 16, column : column + 128].astype(BF)
+
     acc[...] = dot(tokens(), left[...])
-    sa_f[...] = acc[...].astype(BF)
+    in_pieces(sa_f, acc[...])
     pl.semaphore_wait(barrier, len(TENSOR_PEERS) + 1 + len(CHIP_MASKS))
 
-    def part(c):
-        i, h = c // 2, c % 2
-        return i, pl.ds(h * 128, 128)
-
     bit = lambda v, n: lax.rem(lax.shift_right_logical(v, n), 2)
-    near_row = lambda v: pl.multiple_of(32 * (bit(v, 0) + 2 * bit(v, 1) + 4 * bit(v, 4)), 32)
-    far_row = lambda v: pl.multiple_of(16 * bit(v, 2), 16)
-    far_col = lambda v: pl.multiple_of(128 * bit(v, 3), 128)
+    near_row = pl.multiple_of(32 * (bit(s, 0) + 2 * bit(s, 1) + 4 * bit(s, 4)), 32)
+    piece_at = (
+        pl.ds(pl.multiple_of(near_row + 16 * bit(s, 2), 16), 16),
+        pl.ds(pl.multiple_of(128 * bit(s, 3), 128), 128),
+    )
 
     class AllReduce:
-        def __init__(self, total, near_stage, far_stage, near_in, far_in, out):
-            self.total, self.near_stage, self.far_stage = total, near_stage, far_stage
-            self.near_in, self.far_in, self.out = near_in, far_in, out
+        def __init__(self, total, stage, received, out):
+            self.total, self.stage, self.received, self.out = total, stage, received, out
 
         def start(self):
             self.flying = [
-                launch(self.near_stage.at[pl.ds(near_row(s ^ m), 32)], self.near_in.at[n], tensor=s ^ m)
-                for n, m in enumerate(NEAR_GROUP)
+                launch(self.stage.at[s ^ m], self.received.at[n], tensor=s ^ m)
+                for n, m in enumerate(TENSOR_PEERS)
             ]
 
-        def arrived(self):
+        def step(self, n):
             for c in self.flying:
                 c.wait_recv()
-
-        def step(self, n):
-            self.arrived()
-            rows = pl.ds(near_row(s), 32)
-            piece = self.out.at[pl.ds(pl.multiple_of(near_row(s) + far_row(s), 16), 16), pl.ds(far_col(s), 128)]
             if n == 0:
-                part = self.total[rows, :]
-                for m in range(len(NEAR_GROUP)):
-                    part = part + self.near_in[m].astype(F32)
-                self.total[rows, :] = part
-                self.far_stage[...] = part.astype(BF)
-                self.flying = [
-                    launch(
-                        self.far_stage.at[pl.ds(far_row(s ^ m), 16), pl.ds(far_col(s ^ m), 128)],
-                        self.far_in.at[i], tensor=s ^ m,
-                    )
-                    for i, m in enumerate(FAR_GROUP)
-                ]
-            elif n == 1:
-                part = self.total[
-                    pl.ds(pl.multiple_of(near_row(s) + far_row(s), 16), 16), pl.ds(far_col(s), 128)
-                ]
-                for m in range(len(FAR_GROUP)):
-                    part = part + self.far_in[m].astype(F32)
-                piece[...] = part.astype(BF)
-                self.flying = [launch(piece, piece, tensor=s ^ m) for m in FAR_GROUP]
-            elif n == 2:
-                view = self.out.at[rows]
-                self.flying = [launch(view, view, tensor=s ^ m) for m in NEAR_GROUP]
-
-    four = []
-    for c in range(2):
-        i, rows = part(c)
-        four.append(launch(cand.at[i, rows], cand.at[9 + i, rows], tensor=s ^ 4))
-    ar = AllReduce(acc, sa_f, sb_f, ra_f, rb_f, codes)
+                part = self.total[piece_at]
+                for m in range(len(TENSOR_PEERS)):
+                    part = part + self.received[m].astype(F32)
+                self.out[piece_at] = part.astype(BF)
+                view, group = self.out.at[piece_at], FAR_GROUP
+            else:
+                view, group = self.out.at[pl.ds(near_row, 32)], NEAR_GROUP
+            if n < 2:
+                self.flying = [launch(view, view, tensor=s ^ m) for m in group]
+
+    ar = AllReduce(acc, sa_f, ra_f, codes)
     ar.start()
-    for c in range(2, CHUNKS):
-        i, rows = part(c)
-        four.append(launch(cand.at[i, rows], cand.at[9 + i, rows], tensor=s ^ 4))
+
+    four = [launch(cand.at[i], cand.at[9 + i], tensor=s ^ 4) for i in range(MB)]
     own = cand.at[pl.ds(0, MB)]
     sixteen = launch(own, cand.at[pl.ds(15, MB)], tensor=s ^ 16)
     two = launch(own, cand.at[pl.ds(6, MB)], tensor=s ^ 2)
     one = launch(own, cand.at[pl.ds(3, MB)], tensor=s ^ 1)
     relayed = []
 
-    def relay(c):
-        i, rows = part(c)
-        four[c].wait_recv()
-        relayed.append(launch(cand.at[9 + i, rows], cand.at[12 + i, rows], tensor=s ^ 12))
+    def relay(i):
+        four[i].wait_recv()
+        relayed.append(launch(cand.at[9 + i], cand.at[12 + i], tensor=s ^ 12))
 
     def dense(first, last):
         def body(slot, carry):
@@ -219,36 +198,31 @@
 
     pat_load.wait()
     w_load.wait()
-    dense(0, 4)
+    dense(0, 6)
     relay(0)
+    dense(6, 9)
     ar.step(0)
-    dense(4, 8)
+    dense(9, 15)
     relay(1)
-    dense(8, 12)
-    relay(2)
-    ar.step(1)
-    dense(12, 15)
-    relay(3)
     dense(15, 18)
     right_load.wait()
     left_t[...] = left[...].T
-    relay(4)
     right_t[...] = right[...].T
     turned(0, 3)
+    relay(2)
     sixteen.wait_recv()
     turned(15, 18)
-    relay(5)
-    ar.step(2)
+    ar.step(1)
     one.wait_recv()
     two.wait_recv()
     turned(3, 9)
     forward((0, 1, 2, 15, 16, 17, 3, 4, 5, 6, 7, 8), lambda columns: jnp.zeros((TOK, 256), F32))
     turned(9, 12)
     forward((9, 10, 11))
-    ar.step(3)
     gout_load.wait()
-    for c in range(CHUNKS):
-        relayed[c].wait_recv()
+    ar.step(2)
+    for c in relayed:
+        c.wait_recv()
     def activate(n, carry):
         columns = pl.ds(pl.multiple_of(n * 256, 256), 256)
         u = pre[:, columns]
@@ -266,8 +240,8 @@
     lax.fori_loop(0, HID // 256, activate, 0)
 
     acc2[...] = dot(pg[...], right_t[...])
-    sa_b[...] = acc2[...].astype(BF)
-    ar = AllReduce(acc2, sa_b, sb_b, ra_b, rb_b, back)
+    in_pieces(sa_b, acc2[...])
+    ar = AllReduce(acc2, sa_b, ra_b, back)
     ar.start()
 
     def term(slot):
@@ -276,9 +250,7 @@
     far = []
     for i in range(MB):
         gsend[12 + i] = term(12 + i).astype(BF)
-        for h in range(2):
-            rows = pl.ds(h * 128, 128)
-            far.append(launch(gsend.at[12 + i, rows], rx.at[12 + i, rows], tensor=s ^ 12))
+        far.append(launch(gsend.at[12 + i], rx.at[12 + i], tensor=s ^ 12))
 
     def near(level, mask):
         def body(i, carry):
@@ -348,11 +320,10 @@
         lax.fori_loop(0, CHIPS, body, 0)
         return spread(lambda c: out.at[c], lambda m: received.at[m])
 
-    def far_relay(c):
-        i, rows = part(c)
-        far[c].wait_recv()
-        gsend[9 + i, rows] = (g4[i, rows] + rx[12 + i, rows].astype(F32)).astype(BF)
-        nears.append(launch(gsend.at[9 + i, rows], rx.at[9 + i, rows], tensor=s ^ 4))
+    def far_relay(i):
+        far[i].wait_recv()
+        gsend[9 + i] = (g4[i] + rx[12 + i].astype(F32)).astype(BF)
+        nears.append(launch(gsend.at[9 + i], rx.at[9 + i], tensor=s ^ 4))
 
     def flat_parts(out, t):
         for c in range(CHIPS):
@@ -362,16 +333,14 @@
 
     turned(12, 15)
     core0 = blocks(0)
-    ar.step(0)
-    far_relay(0)
     core1 = blocks(1)
     flat_parts(tr, (dot(codes[...].T, pg[...]) * grad_scale).astype(BF))
     core_r = launch(tr.at[:, other], tr_rc, dp=d ^ 1)
+    far_relay(0)
     eight0 = blocks_sum(0, core0)
+    ar.step(0)
+    eight1 = blocks_sum(1, core1)
     far_relay(1)
-    ar.step(1)
-    eight1 = blocks_sum(1, core1)
-    far_relay(2)
     eight_r = flat_sum(tr, tr_rc, tr_s, core_r, tr_r)
 
     def g0_body(i, carry):
@@ -379,11 +348,9 @@
         return carry
 
     lax.fori_loop(0, MB, g0_body, 0)
-    far_relay(3)
+    far_relay(2)
+    ar.step(1)
     ar.step(2)
-    far_relay(4)
-    far_relay(5)
-    ar.step(3)
     flat_parts(tl, (dot(back[...].T, tokens()) * grad_scale).astype(BF))
     core_l = launch(tl.at[:, other], tl_rc, dp=d ^ 1)
     low = dot(back[...], left_t[...])
@@ -426,7 +393,7 @@
 def per_device(tokens, w_blocks, pattern, low_left, low_right, grad_out):
     grad_scale = 1.0 / math.sqrt(TOK * lax.axis_size("dp"))
     vmem = pl.BlockSpec(memory_space=pltpu.VMEM)
-    hbm = pl.BlockSpec(memory_space=pl.ANY)
+    hbm = pl.BlockSpec(memory_space=pltpu.HBM)
     V = pltpu.VMEM
     scratch = [
         V((COLS, NNZ, BLOCK, BLOCK), BF), pltpu.SMEM((COLS, NNZ), jnp.int32),
@@ -434,9 +401,8 @@
         V((SLOTS, TOK, BLOCK), BF), V((SLOTS, BLOCK, TOK), BF),
         V((SLOTS, BLOCK, HID), BF), V((SLOTS, HID, BLOCK), BF),
         V((TOK, HID), F32), V((TOK, HID), BF), V((RANK, FEAT), BF), V((HID, RANK), BF),
-        V((TOK, RANK), F32), V((TOK, RANK), F32), V((TOK, RANK), BF), V((TOK, RANK), BF),
-        V((32, RANK), BF), V((32, RANK), BF), V((7, 32, RANK), BF), V((7, 32, RANK), BF),
-        V((3, 16, 128), BF), V((3, 16, 128), BF),
+        V((TOK, RANK), F32), V((TOK, RANK), F32), V((32, 16, 128), BF), V((32, 16, 128), BF),
+        V((31, 16, 128), BF), V((31, 16, 128), BF),
         V((TOK, RANK), BF), V((TOK, RANK), BF),
         V((SLOTS, TOK, BLOCK), BF), V((SLOTS, TOK, BLOCK), BF),
         V((MB, TOK, BLOCK), F32), V((MB, TOK, BLOCK), F32),
@@ -447,11 +413,11 @@
         pltpu.SemaphoreType.DMA((NUM_SEMS,)), pltpu.SemaphoreType.DMA((NUM_SEMS,)),
     ]
     out_shape = (
-        jax.ShapeDtypeStruct((TOK, HID), BF),
-        jax.ShapeDtypeStruct((TOK, FEAT), F32),
-        jax.ShapeDtypeStruct((COLS, 96, BLOCK), F32),
-        jax.ShapeDtypeStruct((16, FEAT), F32),
-        jax.ShapeDtypeStruct((16, HID), F32),
+        V((TOK, HID), BF),
+        V((TOK, FEAT), F32),
+        V((COLS, 96, BLOCK), F32),
+        V((16, FEAT), F32),
+        V((16, HID), F32),
     )
     hidden, gtok, gblk, glt, gright = pl.pallas_call(
         functools.partial(kernel, grad_scale),

time: 121 us -> 118 us (0.975)
  local copies, waits for them, and re-layouts: 7.99 us -> 3.43 us
    unnamed x5, local copies, waits for them, and re-layouts: 7.99 us -> 3.43 us
    pallas_call x1, Pallas kernels: 112 us -> 113 us  [per_device(): pl.pallas_call(functools.partial(kernel, grad_scale), name='pixelfly', ou...]
where the time goes in v3:
time: 118 us
  Pallas kernels  113 us (96%)
  local copies, waits for them, and re-layouts  3.43 us (3%)
    pallas_call x1, Pallas kernels, per_device(): pl.pallas_call(functools.partial(kernel, grad_scale), name='pixelfly', ou...  113 us
    unnamed x5, local copies, waits for them, and re-layouts  3.43 us

profile of v3, /device:TPU:1, one launch (start us, length us, event | category | flops | bytes accessed | tf_op | source)
XLA Modules:
  0.0 117.6 jit_solution(5397749413872383746)
XLA Ops:
  0.6 113.5 %pixelfly.1 = (bf16[256,768]{1,0:T(8,128)(2,1)S(1)}, f32[256,384]{1,0:T(8,128)S(1)}, f32[6,96,128]{2,1,0:T(8,128)S(1)}, f32[16,384]{1,0:T(8,128)S(1)}, f32[16,768]{1,0:T(8,128)S(1)}) custom-call(bf16[256,384]{1,0:T(8,128)(2,1)} %tokens_hbm.1, bf16[6,12,128,128]{3,2,1,0:T(8,128)(2,1)} %bitcast.3, s32[6,12]{1,0:T(8,128)} %pat_hbm.1, ...), custom_call_target="tpu_custom_call" | custom-call | flops 3221225472 | bytes 6291456 | tf_op jit(solution)/shard_map/pixelfly/pallas_call | solution.py:422
  114.1 0.7 copy.16
  114.9 0.6 copy.19
  115.5 0.6 copy.20
  116.1 0.7 copy.18
  116.8 0.7 copy.17

commit v4 on v3

--- a/solution.py
+++ b/solution.py
@@ -58,7 +58,7 @@
     hidden, gtok, gblk, glt, gright,
     w, pat, left, right, gout, load_sem,
     cand, cand_t, wd, wd_t, pre, pg, left_t, right_t,
-    acc, acc2, sa_f, sa_b, ra_f, ra_b,
+    acc, acc2, sa_f, sb_f, ra_f, rb_f, sa_b, ra_b,
     codes, back, gsend, rx, g4, g0,
     tb, tb_rc, tb_s, tb_r, tr, tr_rc, tr_s, tr_r, tl, tl_rc, tl_s, tl_r,
     send_sem, recv_sem,
@@ -77,6 +77,13 @@
         pending.append(c)
         return c
 
+    barrier = pltpu.get_barrier_semaphore()
+    for m in TENSOR_PEERS:
+        pl.semaphore_signal(barrier, inc=1, device_id={"tensor": s ^ m}, device_id_type=MESH)
+    pl.semaphore_signal(barrier, inc=1, device_id={"dp": d ^ 1}, device_id_type=MESH)
+    for m in CHIP_MASKS:
+        pl.semaphore_signal(barrier, inc=1, device_id={"dp": d ^ (2 * m)}, device_id_type=MESH)
+
     def fetch(n, src, dst):
         c = pltpu.make_async_copy(src, dst, load_sem.at[n])
         c.start()
@@ -88,13 +95,6 @@
     w_load = fetch(5, w_hbm, w)
     right_load = fetch(6, right_hbm, right)
     gout_load = fetch(7, gout_hbm, gout)
-    barrier = pltpu.get_barrier_semaphore()
-    for m in TENSOR_PEERS:
-        pl.semaphore_signal(barrier, inc=1, device_id={"tensor": s ^ m}, device_id_type=MESH)
-    pl.semaphore_signal(barrier, inc=1, device_id={"dp": d ^ 1}, device_id_type=MESH)
-    for m in CHIP_MASKS:
-        pl.semaphore_signal(barrier, inc=1, device_id={"dp": d ^ (2 * m)}, device_id_type=MESH)
-
     for c in loads:
         c.wait()
 
@@ -108,7 +108,7 @@
             out[p] = x[row : row + 16, column : column + 128].astype(BF)
 
     acc[...] = dot(tokens(), left[...])
-    in_pieces(sa_f, acc[...])
+    sa_f[...] = acc[...].astype(BF)
     pl.semaphore_wait(barrier, len(TENSOR_PEERS) + 1 + len(CHIP_MASKS))
 
     bit = lambda v, n: lax.rem(lax.shift_right_logical(v, n), 2)
@@ -142,19 +142,70 @@
             if n < 2:
                 self.flying = [launch(view, view, tensor=s ^ m) for m in group]
 
-    ar = AllReduce(acc, sa_f, ra_f, codes)
+    class NearFirst:
+        def __init__(self, total, near_stage, near_in, far_stage, far_in, out):
+            self.total, self.near_stage, self.near_in = total, near_stage, near_in
+            self.far_stage, self.far_in, self.out = far_stage, far_in, out
+
+        def start(self):
+            def row(v):
+                return pl.multiple_of(32 * (bit(v, 0) + 2 * bit(v, 1) + 4 * bit(v, 4)), 32)
+
+            self.flying = [
+                launch(self.near_stage.at[pl.ds(row(s ^ m), 32)], self.near_in.at[n], tensor=s ^ m)
+                for n, m in enumerate(NEAR_GROUP)
+            ]
+
+        def step(self, n):
+            for c in self.flying:
+                c.wait_recv()
+            rows, piece = pl.ds(near_row, 32), self.out.at[piece_at]
+            if n == 0:
+                part = self.total[rows, :]
+                for m in range(len(NEAR_GROUP)):
+                    part = part + self.near_in[m].astype(F32)
+                self.total[rows, :] = part
+                self.far_stage[...] = part.astype(BF)
+                self.flying = []
+                for i, m in enumerate(FAR_GROUP):
+                    at = (
+                        pl.ds(pl.multiple_of(16 * bit(s ^ m, 2), 16), 16),
+                        pl.ds(pl.multiple_of(128 * bit(s ^ m, 3), 128), 128),
+                    )
+                    self.flying.append(launch(self.far_stage.at[at], self.far_in.at[i], tensor=s ^ m))
+            elif n == 1:
+                part = self.total[piece_at]
+                for m in range(len(FAR_GROUP)):
+                    part = part + self.far_in[m].astype(F32)
+                piece[...] = part.astype(BF)
+                self.flying = [launch(piece, piece, tensor=s ^ m) for m in FAR_GROUP]
+            elif n == 2:
+                view = self.out.at[rows]
+                self.flying = [launch(view, view, tensor=s ^ m) for m in NEAR_GROUP]
+
+    four, relayed = [], []
+
+    def part(c):
+        return c // 2, pl.ds((c % 2) * 128, 128)
+
+    def send_four(first, last):
+        for c in range(first, last):
+            i, rows = part(c)
+            four.append(launch(cand.at[i, rows], cand.at[9 + i, rows], tensor=s ^ 4))
+
+    def relay(c):
+        i, rows = part(c)
+        four[c].wait_recv()
+        relayed.append(launch(cand.at[9 + i, rows], cand.at[12 + i, rows], tensor=s ^ 12))
+
+    ar = NearFirst(acc, sa_f, ra_f, sb_f, rb_f, codes)
+    send_four(0, 2)
     ar.start()
-
-    four = [launch(cand.at[i], cand.at[9 + i], tensor=s ^ 4) for i in range(MB)]
+    send_four(2, 6)
     own = cand.at[pl.ds(0, MB)]
     sixteen = launch(own, cand.at[pl.ds(15, MB)], tensor=s ^ 16)
     two = launch(own, cand.at[pl.ds(6, MB)], tensor=s ^ 2)
     one = launch(own, cand.at[pl.ds(3, MB)], tensor=s ^ 1)
-    relayed = []
-
-    def relay(i):
-        four[i].wait_recv()
-        relayed.append(launch(cand.at[9 + i], cand.at[12 + i], tensor=s ^ 12))
 
     def dense(first, last):
         def body(slot, carry):
@@ -198,21 +249,26 @@
 
     pat_load.wait()
     w_load.wait()
-    dense(0, 6)
+    dense(0, 4)
     relay(0)
-    dense(6, 9)
     ar.step(0)
-    dense(9, 15)
+    dense(4, 8)
     relay(1)
+    dense(8, 12)
+    relay(2)
+    ar.step(1)
+    dense(12, 15)
+    relay(3)
     dense(15, 18)
     right_load.wait()
     left_t[...] = left[...].T
+    relay(4)
     right_t[...] = right[...].T
     turned(0, 3)
-    relay(2)
     sixteen.wait_recv()
     turned(15, 18)
-    ar.step(1)
+    relay(5)
+    ar.step(2)
     one.wait_recv()
     two.wait_recv()
     turned(3, 9)
@@ -220,7 +276,7 @@
     turned(9, 12)
     forward((9, 10, 11))
     gout_load.wait()
-    ar.step(2)
+    ar.step(3)
     for c in relayed:
         c.wait_recv()
     def activate(n, carry):
@@ -390,6 +446,15 @@
         c.wait_send()
 
 
+def hand_over(*refs):
+    n = len(refs) // 2
+    copies = [pltpu.make_async_copy(refs[i], refs[n + i], refs[-1].at[i]) for i in range(n)]
+    for c in copies:
+        c.start()
+    for c in copies:
+        c.wait()
+
+
 def per_device(tokens, w_blocks, pattern, low_left, low_right, grad_out):
     grad_scale = 1.0 / math.sqrt(TOK * lax.axis_size("dp"))
     vmem = pl.BlockSpec(memory_space=pltpu.VMEM)
@@ -401,8 +466,8 @@
         V((SLOTS, TOK, BLOCK), BF), V((SLOTS, BLOCK, TOK), BF),
         V((SLOTS, BLOCK, HID), BF), V((SLOTS, HID, BLOCK), BF),
         V((TOK, HID), F32), V((TOK, HID), BF), V((RANK, FEAT), BF), V((HID, RANK), BF),
-        V((TOK, RANK), F32), V((TOK, RANK), F32), V((32, 16, 128), BF), V((32, 16, 128), BF),
-        V((31, 16, 128), BF), V((31, 16, 128), BF),
+        V((TOK, RANK), F32), V((TOK, RANK), F32), V((TOK, RANK), BF), V((32, RANK), BF),
+        V((7, 32, RANK), BF), V((3, 16, 128), BF), V((32, 16, 128), BF), V((31, 16, 128), BF),
         V((TOK, RANK), BF), V((TOK, RANK), BF),
         V((SLOTS, TOK, BLOCK), BF), V((SLOTS, TOK, BLOCK), BF),
         V((MB, TOK, BLOCK), F32), V((MB, TOK, BLOCK), F32),
@@ -419,7 +484,7 @@
         V((16, FEAT), F32),
         V((16, HID), F32),
     )
-    hidden, gtok, gblk, glt, gright = pl.pallas_call(
+    results = pl.pallas_call(
         functools.partial(kernel, grad_scale),
         name="pixelfly",
         out_shape=out_shape,
@@ -431,6 +496,14 @@
         ),
         cost_estimate=pl.CostEstimate(flops=3 << 30, bytes_accessed=6 << 20, transcendentals=TOK * HID),
     )(tokens, w_blocks.reshape(COLS, NNZ, BLOCK, BLOCK), pattern, low_left, low_right, grad_out)
+    hidden, gtok, gblk, glt, gright = pl.pallas_call(
+        hand_over,
+        name="hand_over",
+        out_shape=[jax.ShapeDtypeStruct(r.shape, r.dtype) for r in results],
+        in_specs=[vmem] * len(results),
+        out_specs=[pl.BlockSpec(memory_space=pl.ANY)] * len(results),
+        scratch_shapes=[pltpu.SemaphoreType.DMA((len(results),))],
+    )(*results)
     return hidden, gtok, gblk, glt.T, gright
 
 

time: 118 us -> 119 us (level)
    pallas_call x0 -> x1, Pallas kernels: none -> 2.24 us  [per_device(): pl.pallas_call(hand_over, name='hand_over', out_shape=[jax.ShapeDtypeStru...]
    pallas_call x1, Pallas kernels: 113 us -> 112 us  [per_device(): pl.pallas_call(functools.partial(kernel, grad_scale), name='pixelfly', ou...]
    unnamed x5 -> x10, local copies, waits for them, and re-layouts: 3.43 us -> 3.43 us
where the time goes in v4:
time: 119 us; the launch traced here: 118 us
  Pallas kernels  114 us (96%)
  local copies, waits for them, and re-layouts  3.43 us (3%)
    pallas_call x1, Pallas kernels, per_device(): pl.pallas_call(functools.partial(kernel, grad_scale), name='pixelfly', ou...  112 us
    unnamed x10, local copies, waits for them, and re-layouts  3.43 us

profile of v4, /device:TPU:1, one launch (start us, length us, event | category | flops | bytes accessed | tf_op | source)
XLA Modules:
  0.0 118.4 jit_solution(2381341689102677887)
XLA Ops:
  0.6 112.1 %pixelfly.1 = (bf16[256,768]{1,0:T(8,128)(2,1)S(1)}, f32[256,384]{1,0:T(8,128)S(1)}, f32[6,96,128]{2,1,0:T(8,128)S(1)}, f32[16,384]{1,0:T(8,128)S(1)}, f32[16,768]{1,0:T(8,128)S(1)}) custom-call(bf16[256,384]{1,0:T(8,128)(2,1)} %tokens_hbm.1, bf16[6,12,128,128]{3,2,1,0:T(8,128)(2,1)} %bitcast.2, s32[6,12]{1,0:T(8,128)} %pat_hbm.1, ...), custom_call_target="tpu_custom_call" | custom-call | flops 3221225472 | bytes 6291456 | tf_op jit(solution)/shard_map/pixelfly/pallas_call | solution.py:487
  112.7 0.0 copy-start
  112.7 0.7 copy-done
  113.5 0.0 copy-start.1
  113.5 0.8 copy-done.1
  114.2 0.0 copy-start.2
  114.2 0.7 copy-done.2
  114.9 0.0 copy-start.3
  114.9 0.6 copy-done.3
  115.6 0.0 copy-start.4
  115.6 0.6 copy-done.4
  116.2 2.2 %hand_over.1 = (bf16[256,768]{1,0:T(8,128)(2,1)}, f32[256,384]{1,0:T(8,128)}, f32[6,96,128]{2,1,0:T(8,128)}, f32[16,384]{1,0:T(8,128)}, f32[16,768]{1,0:T(8,128)}) custom-call(bf16[256,768]{1,0:T(8,128)(2,1)} %copy-done, f32[256,384]{1,0:T(8,128)} %copy-done.1, f32[6,96,128]{2,1,0:T(8,128)} %copy-done.2, f32[16,384]{1,0:T(8,128)} %copy-done.4, ...), custom_call_target="tpu_custom_call" | custom-call | tf_op jit(solution)/shard_map/hand_over/pallas_call | solution.py:499
Async XLA Ops:
  112.7 0.8 copy-start
  113.5 0.8 copy-start.1
  114.2 0.7 copy-start.2
  114.9 0.6 copy-start.3
  115.6 0.6 copy-start.4

commit v5 on v2

--- a/solution.py
+++ b/solution.py
@@ -24,9 +24,9 @@
 GROUPS = 2
 GCOLS = COLS // GROUPS
 CHIPS = 8
-NEAR_GROUP = (1, 2, 3, 16, 17, 18, 19)
-FAR_GROUP = (4, 8, 12)
-TENSOR_PEERS = NEAR_GROUP + FAR_GROUP
+NEAR_GROUP = (19, 18, 17, 16, 3, 2, 1)
+FAR_GROUP = (8, 4, 12)
+TENSOR_PEERS = FAR_GROUP + NEAR_GROUP
 CHIP_MASKS = tuple(range(1, CHIPS))
 GELU_C = math.sqrt(2.0 / math.pi)
 GELU_A = 0.044715
@@ -426,7 +426,7 @@
 def per_device(tokens, w_blocks, pattern, low_left, low_right, grad_out):
     grad_scale = 1.0 / math.sqrt(TOK * lax.axis_size("dp"))
     vmem = pl.BlockSpec(memory_space=pltpu.VMEM)
-    hbm = pl.BlockSpec(memory_space=pl.ANY)
+    hbm = pl.BlockSpec(memory_space=pltpu.HBM)
     V = pltpu.VMEM
     scratch = [
         V((COLS, NNZ, BLOCK, BLOCK), BF), pltpu.SMEM((COLS, NNZ), jnp.int32),
@@ -447,11 +447,11 @@
         pltpu.SemaphoreType.DMA((NUM_SEMS,)), pltpu.SemaphoreType.DMA((NUM_SEMS,)),
     ]
     out_shape = (
-        jax.ShapeDtypeStruct((TOK, HID), BF),
-        jax.ShapeDtypeStruct((TOK, FEAT), F32),
-        jax.ShapeDtypeStruct((COLS, 96, BLOCK), F32),
-        jax.ShapeDtypeStruct((16, FEAT), F32),
-        jax.ShapeDtypeStruct((16, HID), F32),
+        V((TOK, HID), BF),
+        V((TOK, FEAT), F32),
+        V((COLS, 96, BLOCK), F32),
+        V((16, FEAT), F32),
+        V((16, HID), F32),
     )
     hidden, gtok, gblk, glt, gright = pl.pallas_call(
         functools.partial(kernel, grad_scale),

time: 121 us -> 115 us (0.950)
  local copies, waits for them, and re-layouts: 7.99 us -> 3.43 us
    unnamed x5, local copies, waits for them, and re-layouts: 7.99 us -> 3.43 us
where the time goes in v5:
time: 115 us
  Pallas kernels  111 us (97%)
  local copies, waits for them, and re-layouts  3.43 us (3%)
    pallas_call x1, Pallas kernels, per_device(): pl.pallas_call(functools.partial(kernel, grad_scale), name='pixelfly', ou...  111 us
    unnamed x5, local copies, waits for them, and re-layouts  3.43 us

profile of v5, /device:TPU:1, one launch (start us, length us, event | category | flops | bytes accessed | tf_op | source)
XLA Modules:
  0.0 115.0 jit_solution(12703605929772953646)
XLA Ops:
  0.6 110.9 %pixelfly.1 = (bf16[256,768]{1,0:T(8,128)(2,1)S(1)}, f32[256,384]{1,0:T(8,128)S(1)}, f32[6,96,128]{2,1,0:T(8,128)S(1)}, f32[16,384]{1,0:T(8,128)S(1)}, f32[16,768]{1,0:T(8,128)S(1)}) custom-call(bf16[256,384]{1,0:T(8,128)(2,1)} %tokens_hbm.1, bf16[6,12,128,128]{3,2,1,0:T(8,128)(2,1)} %bitcast.3, s32[6,12]{1,0:T(8,128)} %pat_hbm.1, ...), custom_call_target="tpu_custom_call" | custom-call | flops 3221225472 | bytes 6291456 | tf_op jit(solution)/shard_map/pixelfly/pallas_call | solution.py:456
  111.6 0.7 copy.16
  112.3 0.6 copy.19
  112.9 0.6 copy.20
  113.6 0.7 copy.18
  114.3 0.7 copy.17

commit v6 on v5

--- a/solution.py
+++ b/solution.py
@@ -384,6 +384,7 @@
     far_relay(4)
     far_relay(5)
     ar.step(3)
+    early = list(pending)
     flat_parts(tl, (dot(back[...].T, tokens()) * grad_scale).astype(BF))
     core_l = launch(tl.at[:, other], tl_rc, dp=d ^ 1)
     low = dot(back[...], left_t[...])
@@ -418,8 +419,10 @@
         for level in (1, 2, 3, 5):
             total = total + rx[MB * level + i].astype(F32)
         gtok[:, i * BLOCK : (i + 1) * BLOCK] = total
+    for c in early:
+        c.wait_send()
     sum_flat(tl_s.at[chip], tl_r, eight_l, glt)
-    for c in pending:
+    for c in pending[len(early):]:
         c.wait_send()
 
 

time: 115 us -> 115 us (level)
  no operation moved by 1% of the time
where the time goes in v6:
time: 115 us
  Pallas kernels  111 us (97%)
  local copies, waits for them, and re-layouts  3.43 us (3%)
    pallas_call x1, Pallas kernels, per_device(): pl.pallas_call(functools.partial(kernel, grad_scale), name='pixelfly', ou...  111 us
    unnamed x5, local copies, waits for them, and re-layouts  3.43 us

profile of v6, /device:TPU:1, one launch (start us, length us, event | category | flops | bytes accessed | tf_op | source)
XLA Modules:
  0.0 114.9 jit_solution(5951435895041422472)
XLA Ops:
  0.6 110.8 %pixelfly.1 = (bf16[256,768]{1,0:T(8,128)(2,1)S(1)}, f32[256,384]{1,0:T(8,128)S(1)}, f32[6,96,128]{2,1,0:T(8,128)S(1)}, f32[16,384]{1,0:T(8,128)S(1)}, f32[16,768]{1,0:T(8,128)S(1)}) custom-call(bf16[256,384]{1,0:T(8,128)(2,1)} %tokens_hbm.1, bf16[6,12,128,128]{3,2,1,0:T(8,128)(2,1)} %bitcast.3, s32[6,12]{1,0:T(8,128)} %pat_hbm.1, ...), custom_call_target="tpu_custom_call" | custom-call | flops 3221225472 | bytes 6291456 | tf_op jit(solution)/shard_map/pixelfly/pallas_call | solution.py:459
  111.4 0.7 copy.16
  112.2 0.6 copy.19
  112.8 0.6 copy.20
  113.4 0.7 copy.18
  114.1 0.7 copy.17

commit v7 on v6

--- a/solution.py
+++ b/solution.py
@@ -157,13 +157,10 @@
                 view = self.out.at[rows]
                 self.flying = [launch(view, view, tensor=s ^ m) for m in NEAR_GROUP]
 
-    four = []
-    for c in range(2):
-        i, rows = part(c)
-        four.append(launch(cand.at[i, rows], cand.at[9 + i, rows], tensor=s ^ 4))
     ar = AllReduce(acc, sa_f, sb_f, ra_f, rb_f, codes)
     ar.start()
-    for c in range(2, CHUNKS):
+    four = []
+    for c in range(CHUNKS):
         i, rows = part(c)
         four.append(launch(cand.at[i, rows], cand.at[9 + i, rows], tensor=s ^ 4))
     own = cand.at[pl.ds(0, MB)]

time: 115 us -> 115 us (level)
  no operation moved by 1% of the time
where the time goes in v7:
time: 115 us
  Pallas kernels  110 us (96%)
  local copies, waits for them, and re-layouts  3.43 us (3%)
    pallas_call x1, Pallas kernels, per_device(): pl.pallas_call(functools.partial(kernel, grad_scale), name='pixelfly', ou...  110 us
    unnamed x5, local copies, waits for them, and re-layouts  3.43 us

profile of v7, /device:TPU:1, one launch (start us, length us, event | category | flops | bytes accessed | tf_op | source)
XLA Modules:
  0.0 114.5 jit_solution(18082260940011572600)
XLA Ops:
  0.6 110.4 %pixelfly.1 = (bf16[256,768]{1,0:T(8,128)(2,1)S(1)}, f32[256,384]{1,0:T(8,128)S(1)}, f32[6,96,128]{2,1,0:T(8,128)S(1)}, f32[16,384]{1,0:T(8,128)S(1)}, f32[16,768]{1,0:T(8,128)S(1)}) custom-call(bf16[256,384]{1,0:T(8,128)(2,1)} %tokens_hbm.1, bf16[6,12,128,128]{3,2,1,0:T(8,128)(2,1)} %bitcast.3, s32[6,12]{1,0:T(8,128)} %pat_hbm.1, ...), custom_call_target="tpu_custom_call" | custom-call | flops 3221225472 | bytes 6291456 | tf_op jit(solution)/shard_map/pixelfly/pallas_call | solution.py:456
  111.1 0.7 copy.16
  111.8 0.6 copy.19
  112.4 0.6 copy.20
  113.1 0.7 copy.18
  113.8 0.7 copy.17
